TPU v7x, 32 devices: a whole 2x2x4 slice. The times are simulated.
32 devices in a mesh: dp: 8 (over z, y), seq: 4 (over x, core).
Axes of the slice: x: 2, y: 2, z: 4, core: 2. Of those that a mesh axis runs over, the one named last changes fastest.
Arguments:
- queries: bfloat16 [8, 1024, 4096], P('dp', 'seq'), may hold values from -12 to 12
- key_states: bfloat16 [8, 1024, 512], P('dp', 'seq'), may hold values from -12 to 12
- value_states: bfloat16 [8, 1024, 512], P('dp', 'seq'), may hold values from -6 to 6
- out_grad: bfloat16 [8, 1024, 4096], P('dp', 'seq'), may hold values from -6 to 6
- layer_input: bfloat16 [8, 1024, 8192], P('dp', 'seq'), may hold values from -6 to 6
- lengths: int32 [8, 8], P('dp'), may hold values from 1 to 512, 1024 in all within a row
Outputs:
- query_grad: bfloat16 [8, 1024, 4096], P('dp', 'seq')
- key_grad: bfloat16 [8, 1024, 512], P('dp', 'seq')
- value_grad: bfloat16 [8, 1024, 512], P('dp', 'seq')
- value_weight_grad: float32 [8192, 512], P(('dp', 'seq'))
Inputs may be any that keep to these rules, and one draw needn't show every extreme that they name: `lengths`: each row sums to 1024 and its largest entry is exactly 512.
All inputs are finite; a program needn't handle non-finite values.
Results may differ from a plain program's by a relative error of at most 0.018.
Values may be sent and summed in bfloat16 or wider, within the bound.
A program may use at most 192 MiB of HBM per device.

v0:
```python
import functools
import math

import jax
import jax.numpy as jnp
from jax import lax
from jax.experimental import pallas as pl
from jax.experimental.pallas import tpu as pltpu
from jax.sharding import PartitionSpec as P

HD = 128
MOST = 512
SUB = 128
NEG = -1e30


def attention_kernel(
    prior, group, q_ref, g_ref, k_ref, v_ref, sq_ref, sk_ref,
    dq_ref, dkp_ref, dvp_ref, dko_ref, dvo_ref, bias, dk, dv,
):
    local_len = q_ref.shape[0]
    window = k_ref.shape[0]
    span = MOST + SUB
    scale = HD ** (-0.5)
    exp_scale = scale * math.log2(math.e)

    @pl.when(pl.program_id(0) == 0)
    def _():
        key_pos = lax.broadcasted_iota(jnp.int32, (window, local_len), 0) - prior
        row_pos = lax.broadcasted_iota(jnp.int32, (window, local_len), 1)
        allowed = (sk_ref[...] == sq_ref[...]) & (key_pos <= row_pos)
        bias[...] = jnp.where(allowed, 0.0, NEG)

    dk[...] = jnp.zeros_like(dk)
    dv[...] = jnp.zeros_like(dv)
    nt = (((1,), (1,)), ((), ()))
    for r in range(local_len // SUB):
        rows = slice(r * SUB, (r + 1) * SUB)
        start = prior - MOST + r * SUB
        keys = slice(start, start + span)
        k = k_ref[keys, :]
        v = v_ref[keys, :]
        kt = k.T
        part_bias = bias[keys, rows]
        part_bias = jnp.concatenate([part_bias, part_bias], axis=1)
        for pair in range(group // 2):
            a = slice(2 * pair * HD, (2 * pair + 1) * HD)
            b = slice((2 * pair + 1) * HD, (2 * pair + 2) * HD)
            q = jnp.concatenate([q_ref[rows, a], q_ref[rows, b]], axis=0)
            g = jnp.concatenate([g_ref[rows, a], g_ref[rows, b]], axis=0)
            s = lax.dot_general(k, q, nt, preferred_element_type=jnp.float32)
            s = s * exp_scale + part_bias
            e = jnp.exp2(s - jnp.max(s, axis=0, keepdims=True))
            inv = 1.0 / jnp.sum(e, axis=0, keepdims=True)
            dp = lax.dot_general(v, g, nt, preferred_element_type=jnp.float32)
            p = e * inv
            delta = jnp.sum(p * dp, axis=0, keepdims=True)
            ds = (p * ((dp - delta) * scale)).astype(jnp.bfloat16)
            dv[keys, :] += jnp.dot(p.astype(jnp.bfloat16), g, preferred_element_type=jnp.float32)
            dk[keys, :] += jnp.dot(ds, q, preferred_element_type=jnp.float32)
            dqt = jnp.dot(kt, ds, preferred_element_type=jnp.float32)
            dq_ref[rows, a] = dqt[:, :SUB].T.astype(jnp.bfloat16)
            dq_ref[rows, b] = dqt[:, SUB:].T.astype(jnp.bfloat16)
    dkp_ref[...] = dk[:prior, :].astype(jnp.bfloat16)
    dvp_ref[...] = dv[:prior, :].astype(jnp.bfloat16)
    dko_ref[...] = dk[prior:, :]
    dvo_ref[...] = dv[prior:, :]


def attention_grads(q, g, window_kv, seg_rows, seg_keys):
    local_len, width = q.shape
    window = window_kv.shape[0]
    kv_width = window_kv.shape[1] // 2
    kv_heads = kv_width // HD
    group = width // HD // kv_heads
    prior = window - local_len
    wide = lambda n, w: pl.BlockSpec((n, w), lambda i: (0, i))
    whole = lambda s: pl.BlockSpec(s, lambda i: (0, 0))
    elements = window * local_len * kv_heads * group
    return pl.pallas_call(
        functools.partial(attention_kernel, prior, group),
        grid=(kv_heads,),
        in_specs=[
            wide(local_len, group * HD),
            wide(local_len, group * HD),
            wide(window, HD),
            pl.BlockSpec((window, HD), lambda i: (0, i + kv_heads)),
            whole((1, local_len)),
            whole((window, 1)),
        ],
        out_specs=[
            wide(local_len, group * HD),
            wide(prior, HD),
            wide(prior, HD),
            wide(local_len, HD),
            wide(local_len, HD),
        ],
        out_shape=[
            jax.ShapeDtypeStruct((local_len, width), jnp.bfloat16),
            jax.ShapeDtypeStruct((prior, kv_width), jnp.bfloat16),
            jax.ShapeDtypeStruct((prior, kv_width), jnp.bfloat16),
            jax.ShapeDtypeStruct((local_len, kv_width), jnp.float32),
            jax.ShapeDtypeStruct((local_len, kv_width), jnp.float32),
        ],
        scratch_shapes=[
            pltpu.VMEM((window, local_len), jnp.float32),
            pltpu.VMEM((window, HD), jnp.float32),
            pltpu.VMEM((window, HD), jnp.float32),
        ],
        compiler_params=pltpu.CompilerParams(vmem_limit_bytes=40 * 1024 * 1024),
        cost_estimate=pl.CostEstimate(
            flops=10 * elements * HD, bytes_accessed=10 * 1024 * 1024, transcendentals=elements
        ),
    )(q, g, window_kv, window_kv, seg_rows, seg_keys)


def shards(queries, key_states, value_states, out_grad, layer_input, lengths):
    seq_count = lax.axis_size("seq")
    dp_count = lax.axis_size("dp")
    me = lax.axis_index("seq")
    streams, local_len, query_width = queries.shape
    kv_width = key_states.shape[2]
    width = layer_input.shape[2]
    full_len = local_len * seq_count
    steps = -(-MOST // local_len)
    prior = steps * local_len
    piece = width // (dp_count * seq_count)

    own_kv = jnp.concatenate([key_states, value_states], axis=2)
    shifted = [
        lax.ppermute(own_kv, "seq", [(i, i + s) for i in range(seq_count - s)])
        if s < seq_count else jnp.zeros_like(own_kv)
        for s in range(steps, 0, -1)
    ]

    split_input = layer_input.reshape(streams * local_len, dp_count, seq_count, piece)

    def columns_of(owner):
        block = lax.dynamic_slice_in_dim(split_input, owner, 1, axis=2)
        return block.reshape(streams * local_len, dp_count * piece)

    def ring(s):
        return [(i, (i + s) % seq_count) for i in range(seq_count)]

    inputs = [columns_of(me)] + [
        lax.ppermute(columns_of(lax.rem(me + s, seq_count)), "seq", ring(s))
        for s in range(1, seq_count)
    ]
    all_inputs = jnp.concatenate(inputs, axis=0)

    positions = jnp.arange(full_len, dtype=jnp.int32)
    samples = jnp.arange(lengths.shape[1], dtype=jnp.int32)
    ends = jnp.sum(jnp.where(samples[None, :] <= samples[:, None], lengths[:, None, :], 0), axis=2)
    segments = jnp.sum((ends[:, None, :] <= positions[None, :, None]).astype(jnp.int32), axis=2)
    padded = jnp.concatenate([jnp.full((streams, prior), -1, jnp.int32), segments], axis=1)
    seg_window = lax.dynamic_slice_in_dim(padded, me * local_len, prior + local_len, axis=1)

    window_kv = jnp.concatenate(shifted + [own_kv], axis=1)
    results = [
        attention_grads(
            queries[i], out_grad[i], window_kv[i],
            seg_window[i, prior:].reshape(1, local_len), seg_window[i].reshape(-1, 1),
        )
        for i in range(streams)
    ]
    query_grad, key_prior, value_prior, key_own, value_own = (jnp.stack(x) for x in zip(*results))

    def collect(own, parts):
        total = own
        for n, s in enumerate(range(steps, 0, -1)):
            if s < seq_count:
                block = parts[:, n * local_len:(n + 1) * local_len]
                total = total + lax.ppermute(
                    block, "seq", [(i + s, i) for i in range(seq_count - s)]
                ).astype(jnp.float32)
        return total.astype(jnp.bfloat16)

    value_grad = collect(value_own, value_prior)
    key_grad = collect(key_own, key_prior)

    flat_value = value_grad.reshape(streams * local_len, kv_width)
    all_values = jnp.concatenate(
        [flat_value] + [lax.ppermute(flat_value, "seq", ring(s)) for s in range(1, seq_count)],
        axis=0,
    )
    partial = lax.dot_general(
        all_inputs, all_values, (((0,), (0,)), ((), ())), preferred_element_type=jnp.float32
    ) / math.sqrt(streams * dp_count * full_len)
    weight_grad = lax.psum_scatter(
        partial.astype(jnp.bfloat16), "dp", scatter_dimension=0, tiled=True
    ).astype(jnp.float32)
    return (query_grad, key_grad, value_grad, weight_grad)


def solution(mesh):
    token = P("dp", "seq", None)
    return jax.shard_map(
        shards,
        mesh=mesh,
        in_specs=(token, token, token, token, token, P("dp", None)),
        out_specs=(token, token, token, P(("dp", "seq"), None)),
        check_vma=False,
    )
```

profile of v0, /device:TPU:3, one launch (start us, length us, event | category | flops | bytes accessed | tf_op | source)
XLA Modules:
  0.0 178.0 jit_solution(15603804418913600693)
XLA Ops:
  7.2 0.0 reduce-scatter.2.cloned.1.call-start
  7.2 1.0 constant_dynamic-update-slice_fusion.1
  8.2 1.0 constant_dynamic-update-slice_fusion
  9.2 1.3 collective-permute-start.1
  10.5 1.3 collective-permute-start
  11.8 6.4 %copy.14 = bf16[1,256,8192]{1,2,0:T(8,128)(2,1)} copy(bf16[1,256,8192]{2,1,0:T(8,128)(2,1)} %param.10) | data formatting | bytes 8388608 | tf_op args[4]
  18.2 0.0 copy-start.4
  18.2 4.2 %constant_dynamic-slice_fusion.3 = (bf16[256,8,1,256]{0,3,2,1:T(8,128)(2,1)}, bf16[256,8,1,256]{0,3,2,1:T(8,128)(2,1)}, bf16[256,8,1,256]{0,3,2,1:T(8,128)(2,1)}, bf16[256,8,1,256]{0,3,2,1:T(8,128)(2,1)}) fusion(bf16[256,8,4,256]{0,3,2,1:T(8,128)(2,1)} %bitcast.33, s32[]{:T(128)S(6)} %select_n.29, s32[]{:T(128)S(6)} %select_n.32, s32[]{:T(128)S(6)} %select_n.31, ...), kind=kLoop, calls=%fused_computation.35 | loop fusion | bytes 8388624 | tf_op jit(solution)/shard_map/dynamic_slice | solution.py:139
  22.4 1.3 collective-permute-start.8
  23.7 3.1 %collective-permute-start.7 = (bf16[256,2048]{0,1:T(8,128)(2,1)}, bf16[256,2048]{0,1:T(8,128)(2,1)}, u32[]{:S(2)}, u32[]{:S(2)}) collective-permute-start(bf16[256,2048]{0,1:T(8,128)(2,1)} %bitcast.14), channel_id=1, source_target_pairs={{0,2},{1,3},{2,0},{3,1},{4,6},{5,7},{6,4},{7,5},{8,10},{9,11},{10,... | collective-permute-start | bytes 3145736 | tf_op jit(solution)/shard_map/ppermute | solution.py:146
  26.9 1.0 collective-permute-start.6
  27.9 0.0 copy-done.4
  27.9 0.1 select_reduce_fusion
  28.0 0.1 convert_reduce_fusion
  28.1 0.2 copy.13.sk_ref
  28.3 0.0 collective-permute-done.1
  28.3 5.3 %collective-permute-done = bf16[1,256,1024]{2,1,0:T(8,128)(2,1)} collective-permute-done((bf16[1,256,1024]{2,1,0:T(8,128)(2,1)S(1)}, bf16[1,256,1024]{2,1,0:T(8,128)(2,1)}, u32[]{:S(2)}, u32[]{:S(2)}) %collective-permute-start) | collective-permute-done | bytes 524320 | tf_op jit(solution)/shard_map/ppermute | solution.py:131
  33.6 1.2 maximum_bitcast_fusion.k_ref.v_ref
  34.8 0.0 copy-done
  34.8 0.0 copy-start.1
  34.8 1.6 copy-done.1
  36.4 27.3 %shard_map.93 = (bf16[256,4096]{1,0:T(8,128)(2,1)}, bf16[512,512]{1,0:T(8,128)(2,1)S(1)}, bf16[512,512]{1,0:T(8,128)(2,1)S(1)}, f32[256,512]{1,0:T(8,128)S(1)}, f32[256,512]{1,0:T(8,128)S(1)}) custom-call(bf16[256,4096]{1,0:T(8,128)(2,1)S(1)} %bitcast.31, bf16[256,4096]{1,0:T(8,128)(2,1)S(1)} %bitcast.32, ...), custom_call_target="tpu_custom_call" | custom-call | flops 8053063680 | bytes 10485760 | tf_op jit(solution)/shard_map/pallas_call | solution.py:80
  63.7 1.3 collective-permute-start.5
  65.0 2.0 %collective-permute-start.4 = (bf16[1,256,512]{2,1,0:T(8,128)(2,1)S(1)}, bf16[1,256,512]{2,1,0:T(8,128)(2,1)S(1)}, u32[]{:S(2)}, u32[]{:S(2)}) collective-permute-start(bf16[1,256,512]{2,1,0:T(8,128)(2,1)S(1)} %get-tuple-element.18), channel_id=1, source_target_pairs={{2,0},{3,1},{6,4},{7,5},{10,8},{11,9},{14,12},{15,13},{18,16},{19,... | collective-permute-start | bytes 786440 | tf_op jit(solution)/shard_map/ppermute | solution.py:173
  67.0 0.0 collective-permute-done.5
  67.0 11.0 %collective-permute-done.4 = bf16[1,256,512]{2,1,0:T(8,128)(2,1)S(1)} collective-permute-done((bf16[1,256,512]{2,1,0:T(8,128)(2,1)S(1)}, bf16[1,256,512]{2,1,0:T(8,128)(2,1)S(1)}, u32[]{:S(2)}, u32[]{:S(2)}) %collective-permute-start.4) | collective-permute-done | bytes 262176 | tf_op jit(solution)/shard_map/ppermute | solution.py:173
  78.1 0.1 fusion.18
  78.2 0.0 copy-start.3
  78.2 2.9 %collective-permute-start.11 = (bf16[256,512]{1,0:T(8,128)(2,1)S(1)}, bf16[256,512]{1,0:T(8,128)(2,1)S(1)}, u32[]{:S(2)}, u32[]{:S(2)}) collective-permute-start(bf16[256,512]{1,0:T(8,128)(2,1)S(1)} %bitcast.35), channel_id=1, source_target_pairs={{0,3},{1,0},{2,1},{3,2},{4,7},{5,4},{6,5},{7,6},{8,11},{9,8},{10,9... | collective-permute-start | bytes 786440 | tf_op jit(solution)/shard_map/ppermute | solution.py:183
  81.1 2.2 %collective-permute-start.10 = (bf16[256,512]{1,0:T(8,128)(2,1)S(1)}, bf16[256,512]{1,0:T(8,128)(2,1)S(1)}, u32[]{:S(2)}, u32[]{:S(2)}) collective-permute-start(bf16[256,512]{1,0:T(8,128)(2,1)S(1)} %bitcast.36), channel_id=1, source_target_pairs={{0,2},{1,3},{2,0},{3,1},{4,6},{5,7},{6,4},{7,5},{8,10},{9,11},{10,... | collective-permute-start | bytes 786440 | tf_op jit(solution)/shard_map/ppermute | solution.py:183
  83.3 0.0 collective-permute-done.8
  83.3 0.0 collective-permute-start.9
  83.3 0.0 collective-permute-done.7
  83.3 0.0 collective-permute-done.6
  83.3 7.0 %collective-permute-done.11 = bf16[256,512]{1,0:T(8,128)(2,1)S(1)} collective-permute-done((bf16[256,512]{1,0:T(8,128)(2,1)S(1)}, bf16[256,512]{1,0:T(8,128)(2,1)S(1)}, u32[]{:S(2)}, u32[]{:S(2)}) %collective-permute-start.11) | collective-permute-done | bytes 262176 | tf_op jit(solution)/shard_map/ppermute | solution.py:183
  90.3 0.0 collective-permute-done.10
  90.3 2.7 %collective-permute-done.9 = bf16[256,512]{1,0:T(8,128)(2,1)S(1)} collective-permute-done((bf16[256,512]{1,0:T(8,128)(2,1)S(1)}, bf16[256,512]{1,0:T(8,128)(2,1)S(1)}, u32[]{:S(2)}, u32[]{:S(2)}) %collective-permute-start.9) | collective-permute-done | bytes 262176 | tf_op jit(solution)/shard_map/ppermute | solution.py:183
  93.0 0.0 copy-done.2
  93.0 5.5 %multiply_convert_fusion = bf16[2048,512]{1,0:T(8,128)(2,1)} fusion(bf16[256,2048]{0,1:T(8,128)(2,1)} %collective-permute-done.8, bf16[256,2048]{0,1:T(8,128)(2,1)} %collective-permute-done.7, bf16[256,2048]{0,1:T(8,128)(2,1)} %collective-permute-done.6, bf16[256,2048]{0,1:T(8,128)(2,1)S(1)} %bitcast.34, bf16[256,512]{1,0:T(8,128)(2,1)S(1)} %collective-permute-done.11, ...), kind=kOutput, calls=%fused_computation.8 | convolution fusion | flops 2170552320 | bytes 7340032 | tf_op jit(solution)/shard_map/dot_general | solution.py:186
  98.5 0.0 copy-done.3
  98.5 0.0 reduce-scatter.2.cloned.1.call-update
  98.6 5.1 %collective-permute-start.3 = (bf16[1,256,512]{2,1,0:T(8,128)(2,1)S(1)}, bf16[1,256,512]{2,1,0:T(8,128)(2,1)S(1)}, u32[]{:S(2)}, u32[]{:S(2)}) collective-permute-start(bf16[1,256,512]{2,1,0:T(8,128)(2,1)S(1)} %get-tuple-element.21), channel_id=1, source_target_pairs={{1,0},{2,1},{3,2},{5,4},{6,5},{7,6},{9,8},{10,9},{11,10},{13,12},{... | collective-permute-start | bytes 786440 | tf_op jit(solution)/shard_map/ppermute | solution.py:173
  103.7 1.4 collective-permute-start.2
  105.1 0.0 collective-permute-done.3
  105.1 6.1 %collective-permute-done.2 = bf16[1,256,512]{2,1,0:T(8,128)(2,1)S(1)} collective-permute-done((bf16[1,256,512]{2,1,0:T(8,128)(2,1)S(1)}, bf16[1,256,512]{2,1,0:T(8,128)(2,1)S(1)}, u32[]{:S(2)}, u32[]{:S(2)}) %collective-permute-start.2) | collective-permute-done | bytes 262176 | tf_op jit(solution)/shard_map/ppermute | solution.py:173
  111.2 0.8 fusion.20
  112.0 57.3 %reduce-scatter.2.cloned.1.call-done = bf16[256,512]{1,0:T(8,128)(2,1)} async-done(((bf16[2048,512]{1,0:T(8,128)(2,1)}), bf16[256,512]{1,0:T(8,128)(2,1)}) %reduce-scatter.2.cloned.1.call-update) | async-done | bytes 262160 | tf_op jit(solution)/shard_map/reduce_scatter | solution.py:189
  169.3 1.8 %convert_element_type.43 = f32[256,512]{1,0:T(8,128)} convert(bf16[256,512]{1,0:T(8,128)(2,1)} %reduce-scatter.2.cloned.1.call-done) | non-fusion elementwise | flops 131072 | bytes 786432 | tf_op jit(solution)/shard_map/convert_element_type | solution.py:191
  (6 shorter events, 0.1 us)
Async XLA Ops:
  7.2 162.2 %reduce-scatter.2.cloned.1.call-start = ((), (), s32[]{:S(2)}) async-start(), calls=%async_computation.1 | async-start | bytes 2359296 | tf_op jit(solution)/shard_map/reduce_scatter | solution.py:189
  9.2 19.1 %collective-permute-start.1 = (bf16[1,256,1024]{2,1,0:T(8,128)(2,1)S(1)}, bf16[1,256,1024]{2,1,0:T(8,128)(2,1)S(1)}, u32[]{:S(2)}, u32[]{:S(2)}) collective-permute-start(bf16[1,256,1024]{2,1,0:T(8,128)(2,1)S(1)} %constant_dynamic-update-slice_fusion), channel_id=1, source_target_pairs={{0,1},{1,2},{2,3},{4,5},{5,6},{6,7},{8,9},{9,10},{10,11},{12,13},{... | collective-permute-start | bytes 1572872 | tf_op jit(solution)/shard_map/ppermute | solution.py:131
  10.5 23.1 %collective-permute-start = (bf16[1,256,1024]{2,1,0:T(8,128)(2,1)S(1)}, bf16[1,256,1024]{2,1,0:T(8,128)(2,1)}, u32[]{:S(2)}, u32[]{:S(2)}) collective-permute-start(bf16[1,256,1024]{2,1,0:T(8,128)(2,1)S(1)} %constant_dynamic-update-slice_fusion), channel_id=1, source_target_pairs={{0,2},{1,3},{4,6},{5,7},{8,10},{9,11},{12,14},{13,15},{16,18},{17,... | collective-permute-start | bytes 1572872 | tf_op jit(solution)/shard_map/ppermute | solution.py:131
  18.2 9.7 %copy-start.4 = (s32[1,8]{1,0:T(1,128)S(1)}, s32[1,8]{1,0:T(1,128)}, u32[]{:S(2)}) copy-start(s32[1,8]{1,0:T(1,128)} %param.11) | copy-start | bytes 100
  22.4 12.3 %copy-start = (bf16[1,256,4096]{2,1,0:T(8,128)(2,1)S(1)}, bf16[1,256,4096]{2,1,0:T(8,128)(2,1)}, u32[]{:S(2)}) copy-start(bf16[1,256,4096]{2,1,0:T(8,128)(2,1)} %param.6) | copy-start | bytes 6291460
  22.4 60.9 %collective-permute-start.8 = (bf16[256,2048]{0,1:T(8,128)(2,1)}, bf16[256,2048]{0,1:T(8,128)(2,1)}, u32[]{:S(2)}, u32[]{:S(2)}) collective-permute-start(bf16[256,2048]{0,1:T(8,128)(2,1)} %bitcast.15), channel_id=1, source_target_pairs={{0,3},{1,0},{2,1},{3,2},{4,7},{5,4},{6,5},{7,6},{8,11},{9,8},{10,9... | collective-permute-start | bytes 3145736 | tf_op jit(solution)/shard_map/ppermute | solution.py:146
  23.7 59.6 %collective-permute-start.7 = (bf16[256,2048]{0,1:T(8,128)(2,1)}, bf16[256,2048]{0,1:T(8,128)(2,1)}, u32[]{:S(2)}, u32[]{:S(2)}) collective-permute-start(bf16[256,2048]{0,1:T(8,128)(2,1)} %bitcast.14), channel_id=1, source_target_pairs={{0,2},{1,3},{2,0},{3,1},{4,6},{5,7},{6,4},{7,5},{8,10},{9,11},{10,... | collective-permute-start | bytes 3145736 | tf_op jit(solution)/shard_map/ppermute | solution.py:146
  26.9 56.5 %collective-permute-start.6 = (bf16[256,2048]{0,1:T(8,128)(2,1)}, bf16[256,2048]{0,1:T(8,128)(2,1)}, u32[]{:S(2)}, u32[]{:S(2)}) collective-permute-start(bf16[256,2048]{0,1:T(8,128)(2,1)} %bitcast.13), channel_id=1, source_target_pairs={{0,1},{1,2},{2,3},{3,0},{4,5},{5,6},{6,7},{7,4},{8,9},{9,10},{10,1... | collective-permute-start | bytes 3145736 | tf_op jit(solution)/shard_map/ppermute | solution.py:146
  34.8 1.6 copy-start.1
  36.4 56.6 %copy-start.2 = (bf16[256,8,1,256]{0,3,2,1:T(8,128)(2,1)S(1)}, bf16[256,8,1,256]{0,3,2,1:T(8,128)(2,1)}, u32[]{:S(2)}) copy-start(bf16[256,8,1,256]{0,3,2,1:T(8,128)(2,1)} %get-tuple-element.14) | copy-start | bytes 3145732
  63.7 3.3 %collective-permute-start.5 = (bf16[1,256,512]{2,1,0:T(8,128)(2,1)S(1)}, bf16[1,256,512]{2,1,0:T(8,128)(2,1)S(1)}, u32[]{:S(2)}, u32[]{:S(2)}) collective-permute-start(bf16[1,256,512]{2,1,0:T(8,128)(2,1)S(1)} %get-tuple-element.19), channel_id=1, source_target_pairs={{1,0},{2,1},{3,2},{5,4},{6,5},{7,6},{9,8},{10,9},{11,10},{13,12},{... | collective-permute-start | bytes 786440 | tf_op jit(solution)/shard_map/ppermute | solution.py:173
  65.0 13.1 %collective-permute-start.4 = (bf16[1,256,512]{2,1,0:T(8,128)(2,1)S(1)}, bf16[1,256,512]{2,1,0:T(8,128)(2,1)S(1)}, u32[]{:S(2)}, u32[]{:S(2)}) collective-permute-start(bf16[1,256,512]{2,1,0:T(8,128)(2,1)S(1)} %get-tuple-element.18), channel_id=1, source_target_pairs={{2,0},{3,1},{6,4},{7,5},{10,8},{11,9},{14,12},{15,13},{18,16},{19,... | collective-permute-start | bytes 786440 | tf_op jit(solution)/shard_map/ppermute | solution.py:173
  78.2 20.4 %copy-start.3 = (bf16[1,256,512]{2,1,0:T(8,128)(2,1)}, bf16[1,256,512]{2,1,0:T(8,128)(2,1)S(1)}, u32[]{:S(2)}) copy-start(bf16[1,256,512]{2,1,0:T(8,128)(2,1)S(1)} %fusion.18) | copy-start | bytes 786436
  78.2 12.1 %collective-permute-start.11 = (bf16[256,512]{1,0:T(8,128)(2,1)S(1)}, bf16[256,512]{1,0:T(8,128)(2,1)S(1)}, u32[]{:S(2)}, u32[]{:S(2)}) collective-permute-start(bf16[256,512]{1,0:T(8,128)(2,1)S(1)} %bitcast.35), channel_id=1, source_target_pairs={{0,3},{1,0},{2,1},{3,2},{4,7},{5,4},{6,5},{7,6},{8,11},{9,8},{10,9... | collective-permute-start | bytes 786440 | tf_op jit(solution)/shard_map/ppermute | solution.py:183
  81.1 9.2 %collective-permute-start.10 = (bf16[256,512]{1,0:T(8,128)(2,1)S(1)}, bf16[256,512]{1,0:T(8,128)(2,1)S(1)}, u32[]{:S(2)}, u32[]{:S(2)}) collective-permute-start(bf16[256,512]{1,0:T(8,128)(2,1)S(1)} %bitcast.36), channel_id=1, source_target_pairs={{0,2},{1,3},{2,0},{3,1},{4,6},{5,7},{6,4},{7,5},{8,10},{9,11},{10,... | collective-permute-start | bytes 786440 | tf_op jit(solution)/shard_map/ppermute | solution.py:183
  83.3 9.7 %collective-permute-start.9 = (bf16[256,512]{1,0:T(8,128)(2,1)S(1)}, bf16[256,512]{1,0:T(8,128)(2,1)S(1)}, u32[]{:S(2)}, u32[]{:S(2)}) collective-permute-start(bf16[256,512]{1,0:T(8,128)(2,1)S(1)} %bitcast.37), channel_id=1, source_target_pairs={{0,1},{1,2},{2,3},{3,0},{4,5},{5,6},{6,7},{7,4},{8,9},{9,10},{10,1... | collective-permute-start | bytes 786440 | tf_op jit(solution)/shard_map/ppermute | solution.py:183
  98.6 6.4 %collective-permute-start.3 = (bf16[1,256,512]{2,1,0:T(8,128)(2,1)S(1)}, bf16[1,256,512]{2,1,0:T(8,128)(2,1)S(1)}, u32[]{:S(2)}, u32[]{:S(2)}) collective-permute-start(bf16[1,256,512]{2,1,0:T(8,128)(2,1)S(1)} %get-tuple-element.21), channel_id=1, source_target_pairs={{1,0},{2,1},{3,2},{5,4},{6,5},{7,6},{9,8},{10,9},{11,10},{13,12},{... | collective-permute-start | bytes 786440 | tf_op jit(solution)/shard_map/ppermute | solution.py:173
  103.7 7.5 %collective-permute-start.2 = (bf16[1,256,512]{2,1,0:T(8,128)(2,1)S(1)}, bf16[1,256,512]{2,1,0:T(8,128)(2,1)S(1)}, u32[]{:S(2)}, u32[]{:S(2)}) collective-permute-start(bf16[1,256,512]{2,1,0:T(8,128)(2,1)S(1)} %get-tuple-element.20), channel_id=1, source_target_pairs={{2,0},{3,1},{6,4},{7,5},{10,8},{11,9},{14,12},{15,13},{18,16},{19,... | collective-permute-start | bytes 786440 | tf_op jit(solution)/shard_map/ppermute | solution.py:173
Sparse Core Ops, SparseCore 0:
  98.7 70.5 reduce-scatter.1
where the time goes:
time: 181 us; the launch traced here: 178 us
  waiting for transfers between devices  89.5 us (49%)
  Pallas kernels  27.3 us (15%)
  starting transfers between devices  22.9 us (13%)
  local copies, waits for them, and re-layouts  14.5 us (8%)
  between operations  14.2 us (8%)
  matrix products  5.54 us (3%)
  other arithmetic  4.08 us (2%)
    reduce_scatter x1, waiting for transfers between devices, shards(): lax.psum_scatter(partial.astype(jnp.bfloat16), 'dp', scatter_dimension=0,...  57.3 us
    pallas_call x1, Pallas kernels, attention_grads(): pl.pallas_call(functools.partial(attention_kernel, prior, group), grid=(k...  27.3 us
    ppermute x4, waiting for transfers between devices, collect(): lax.ppermute(block, 'seq', [(i + s, i) for i in range(seq_count - s)])  17.2 us
    ppermute x4, starting transfers between devices, collect(): lax.ppermute(block, 'seq', [(i + s, i) for i in range(seq_count - s)])  9.72 us
    ppermute x3, waiting for transfers between devices, shards(): lax.ppermute(flat_value, 'seq', ring(s))  9.67 us
    unnamed x12, local copies, waits for them, and re-layouts  8.98 us
    dot_general x1, matrix products, shards(): lax.dot_general(all_inputs, all_values, (((0,), (0,)), ((), ())), preferr...  5.54 us
    ppermute x3, starting transfers between devices, shards(): lax.ppermute(columns_of(lax.rem(me + s, seq_count)), 'seq', ring(s))  5.43 us
  transfers between devices with their start and end apart: 13, of which 6 were waited for; matrix products, arithmetic and copies ran while one was open for 7% of the time, Pallas kernels for 15%

commit v1 on v0

--- a/solution.py
+++ b/solution.py
@@ -133,18 +133,26 @@
         for s in range(steps, 0, -1)
     ]
 
-    split_input = layer_input.reshape(streams * local_len, dp_count, seq_count, piece)
+    both = ("dp", "seq")
+    pair = 2 if dp_count % 2 == 0 else 1
+    members = pair * seq_count
+    groups = dp_count // pair
+    member = lax.rem(lax.axis_index("dp"), pair) * seq_count + me
+    split_input = layer_input.reshape(streams * local_len, groups, members, piece)
 
     def columns_of(owner):
         block = lax.dynamic_slice_in_dim(split_input, owner, 1, axis=2)
-        return block.reshape(streams * local_len, dp_count * piece)
+        return block.reshape(streams * local_len, groups * piece)
 
     def ring(s):
-        return [(i, (i + s) % seq_count) for i in range(seq_count)]
-
-    inputs = [columns_of(me)] + [
-        lax.ppermute(columns_of(lax.rem(me + s, seq_count)), "seq", ring(s))
-        for s in range(1, seq_count)
+        return [
+            (z * members + i, z * members + (i + s) % members)
+            for z in range(groups) for i in range(members)
+        ]
+
+    inputs = [columns_of(member)] + [
+        lax.ppermute(columns_of(lax.rem(member + s, members)), both, ring(s))
+        for s in range(1, members)
     ]
     all_inputs = jnp.concatenate(inputs, axis=0)
 
@@ -180,15 +188,20 @@
 
     flat_value = value_grad.reshape(streams * local_len, kv_width)
     all_values = jnp.concatenate(
-        [flat_value] + [lax.ppermute(flat_value, "seq", ring(s)) for s in range(1, seq_count)],
+        [flat_value] + [lax.ppermute(flat_value, both, ring(s)) for s in range(1, members)],
         axis=0,
     )
     partial = lax.dot_general(
         all_inputs, all_values, (((0,), (0,)), ((), ())), preferred_element_type=jnp.float32
     ) / math.sqrt(streams * dp_count * full_len)
-    weight_grad = lax.psum_scatter(
-        partial.astype(jnp.bfloat16), "dp", scatter_dimension=0, tiled=True
-    ).astype(jnp.float32)
+    mine = lax.axis_index("dp") // pair
+    partial = partial.reshape(groups, piece, kv_width)
+    weight_grad = lax.dynamic_index_in_dim(partial, mine, 0, keepdims=False)
+    halved = partial.astype(jnp.bfloat16)
+    for s in range(1, groups):
+        block = lax.dynamic_index_in_dim(halved, lax.rem(mine + s, groups), 0, keepdims=False)
+        turn = [(i, (i + s * pair) % dp_count) for i in range(dp_count)]
+        weight_grad = weight_grad + lax.ppermute(block, "dp", turn).astype(jnp.float32)
     return (query_grad, key_grad, value_grad, weight_grad)
 
 

time: 181 us -> 149 us (0.82); the launches traced: 178 us -> 148 us
  waiting for transfers between devices: 89.5 us -> 47.6 us
  starting transfers between devices: 22.9 us -> 49.8 us
  between operations: 14.2 us -> 1.11 us
  matrix products: 5.54 us -> 2.33 us
    reduce_scatter x1 -> x0, waiting for transfers between devices: 57.3 us -> none  [shards(): lax.psum_scatter(partial.astype(jnp.bfloat16), 'dp', scatter_dimension=0,...]
    ppermute x6 -> x17, waiting for transfers between devices: 9.67 us -> 46.5 us  [the longest x3 21.8 us: shards(): lax.ppermute(block, 'dp', turn).astype(jnp.float32)]
    ppermute x6 -> x17, starting transfers between devices: 10.6 us -> 37.5 us  [the longest x7 18.1 us: shards(): lax.ppermute(flat_value, both, ring(s))]
    ppermute x4, waiting for transfers between devices: 17.2 us -> 0.01 us  [collect(): lax.ppermute(block, 'seq', [(i + s, i) for i in range(seq_count - s)])]
    ppermute x2, waiting for transfers between devices: 5.29 us -> 1.14 us  [shards(): lax.ppermute(own_kv, 'seq', [(i, i + s) for i in range(seq_count - s)])]
    dot_general x1, matrix products: 5.54 us -> 2.33 us  [shards(): lax.dot_general(all_inputs, all_values, (((0,), (0,)), ((), ())), preferr...]
    add x0 -> x1, other arithmetic: none -> 2.03 us  [shards(): weight_grad + lax.ppermute(block, 'dp', turn).astype(jnp.float32)]
    unnamed x12 -> x27, local copies, waits for them, and re-layouts: 8.98 us -> 7.89 us
  transfers between devices with their start and end apart: 13 -> 23, of which waited for: 6 -> 8; matrix products, arithmetic and copies ran while one was open for 7% -> 12% of each run, Pallas kernels for 15% -> 18%
where the time goes in v1:
time: 149 us; the launch traced here: 148 us
  starting transfers between devices  49.8 us (33%)
  waiting for transfers between devices  47.6 us (32%)
  Pallas kernels  27.3 us (18%)
  local copies, waits for them, and re-layouts  14.8 us (10%)
  other arithmetic  5.39 us (4%)
  matrix products  2.33 us (2%)
    pallas_call x1, Pallas kernels, attention_grads(): pl.pallas_call(functools.partial(attention_kernel, prior, group), grid=(k...  27.3 us
    ppermute x3, waiting for transfers between devices, shards(): lax.ppermute(block, 'dp', turn).astype(jnp.float32)  21.8 us
    ppermute x7, starting transfers between devices, shards(): lax.ppermute(flat_value, both, ring(s))  18.1 us
    ppermute x7, starting transfers between devices, shards(): lax.ppermute(columns_of(lax.rem(member + s, members)), both, ring(s))  15.7 us
    ppermute x7, waiting for transfers between devices, shards(): lax.ppermute(columns_of(lax.rem(member + s, members)), both, ring(s))  15.1 us
    ppermute x4, starting transfers between devices, collect(): lax.ppermute(block, 'seq', [(i + s, i) for i in range(seq_count - s)])  9.68 us
    ppermute x7, waiting for transfers between devices, shards(): lax.ppermute(flat_value, both, ring(s))  9.56 us
    unnamed x27, local copies, waits for them, and re-layouts  7.89 us
  transfers between devices with their start and end apart: 23, of which 8 were waited for; matrix products, arithmetic and copies ran while one was open for 12% of the time, Pallas kernels for 18%

profile of v1, /device:TPU:3, one launch (start us, length us, event | category | flops | bytes accessed | tf_op | source)
XLA Modules:
  0.0 148.3 jit_solution(10903030399856118792)
XLA Ops:
  0.6 1.0 constant_dynamic-update-slice_fusion.1
  1.6 1.0 constant_dynamic-update-slice_fusion
  2.6 1.3 collective-permute-start.1
  3.9 1.3 collective-permute-start
  5.3 6.4 %copy.14 = bf16[1,256,8192]{1,2,0:T(8,128)(2,1)} copy(bf16[1,256,8192]{2,1,0:T(8,128)(2,1)} %param.10) | data formatting | bytes 8388608 | tf_op args[4]
  11.6 4.0 %constant_dynamic-slice_fusion = (bf16[256,4,1,256]{0,3,2,1:T(8,128)(2,1)}, bf16[256,4,1,256]{0,3,2,1:T(8,128)(2,1)}, bf16[256,4,1,256]{0,3,2,1:T(8,128)(2,1)}, ...) fusion(bf16[256,4,8,256]{0,3,2,1:T(8,128)(2,1)} %bitcast.54, ...), kind=kLoop, calls=%fused_computation.38 | loop fusion | bytes 8388640 | tf_op jit(solution)/shard_map/dynamic_slice | solution.py:144
  15.7 4.3 %collective-permute-start.10 = (bf16[256,1024]{0,1:T(8,128)(2,1)}, bf16[256,1024]{0,1:T(8,128)(2,1)S(1)}, u32[]{:S(2)}, u32[]{:S(2)}) collective-permute-start(bf16[256,1024]{0,1:T(8,128)(2,1)} %bitcast.17), channel_id=1, source_target_pairs={{0,5},{1,6},{2,7},{3,0},{4,1},{5,2},{6,3},{7,4},{8,13},{9,14},{10,... | collective-permute-start | bytes 1572872 | tf_op jit(solution)/shard_map/ppermute | solution.py:154
  19.9 1.2 collective-permute-start.9
  21.2 0.1 select_reduce_fusion
  21.3 0.1 convert_reduce_fusion
  21.4 0.2 copy.13.sk_ref
  21.7 0.1 constant_dynamic-update-slice_fusion.9
  21.7 1.5 %collective-permute-start.7 = (bf16[256,1024]{0,1:T(8,128)(2,1)}, bf16[256,1024]{0,1:T(8,128)(2,1)S(1)}, u32[]{:S(2)}, u32[]{:S(2)}) collective-permute-start(bf16[256,1024]{0,1:T(8,128)(2,1)} %bitcast.60), channel_id=1, source_target_pairs={{0,2},{1,3},{2,4},{3,5},{4,6},{5,7},{6,0},{7,1},{8,10},{9,11},{10,... | collective-permute-start | bytes 1572872 | tf_op jit(solution)/shard_map/ppermute | solution.py:154
  23.3 1.1 collective-permute-done
  24.4 1.2 maximum_bitcast_fusion.k_ref.v_ref
  25.6 27.3 %shard_map.93 = (bf16[256,4096]{1,0:T(8,128)(2,1)}, bf16[512,512]{1,0:T(8,128)(2,1)S(1)}, bf16[512,512]{1,0:T(8,128)(2,1)S(1)}, f32[256,512]{1,0:T(8,128)S(1)}, f32[256,512]{1,0:T(8,128)S(1)}) custom-call(bf16[256,4096]{1,0:T(8,128)(2,1)S(1)} %bitcast.52, bf16[256,4096]{1,0:T(8,128)(2,1)S(1)} %bitcast.53, ...), custom_call_target="tpu_custom_call" | custom-call | flops 8053063680 | bytes 10485760 | tf_op jit(solution)/shard_map/pallas_call | solution.py:80
  53.0 2.9 %collective-permute-start.4 = (bf16[1,256,512]{2,1,0:T(8,128)(2,1)S(1)}, bf16[1,256,512]{2,1,0:T(8,128)(2,1)S(1)}, u32[]{:S(2)}, u32[]{:S(2)}) collective-permute-start(bf16[1,256,512]{2,1,0:T(8,128)(2,1)S(1)} %get-tuple-element.27), channel_id=1, source_target_pairs={{2,0},{3,1},{6,4},{7,5},{10,8},{11,9},{14,12},{15,13},{18,16},{19,... | collective-permute-start | bytes 786440 | tf_op jit(solution)/shard_map/ppermute | solution.py:181
  55.8 0.1 constant_dynamic-update-slice_fusion.8
  55.9 0.8 fusion.9
  56.7 1.7 %collective-permute-start.5 = (bf16[1,256,512]{2,1,0:T(8,128)(2,1)S(1)}, bf16[1,256,512]{2,1,0:T(8,128)(2,1)S(1)}, u32[]{:S(2)}, u32[]{:S(2)}) collective-permute-start(bf16[1,256,512]{2,1,0:T(8,128)(2,1)S(1)} %get-tuple-element.28), channel_id=1, source_target_pairs={{1,0},{2,1},{3,2},{5,4},{6,5},{7,6},{9,8},{10,9},{11,10},{13,12},{... | collective-permute-start | bytes 786440 | tf_op jit(solution)/shard_map/ppermute | solution.py:181
  58.5 0.1 constant_dynamic-update-slice_fusion.7
  58.6 7.1 %collective-permute-start.11 = (bf16[256,1024]{0,1:T(8,128)(2,1)S(1)}, bf16[256,1024]{0,1:T(8,128)(2,1)S(1)}, u32[]{:S(2)}, u32[]{:S(2)}) collective-permute-start(bf16[256,1024]{0,1:T(8,128)(2,1)S(1)} %bitcast.59), channel_id=1, source_target_pairs={{0,6},{1,7},{2,0},{3,1},{4,2},{5,3},{6,4},{7,5},{8,14},{9,15},{10,... | collective-permute-start | bytes 1572872 | tf_op jit(solution)/shard_map/ppermute | solution.py:154
  65.7 1.6 %collective-permute-start.12 = (bf16[256,1024]{0,1:T(8,128)(2,1)S(1)}, bf16[256,1024]{0,1:T(8,128)(2,1)S(1)}, u32[]{:S(2)}, u32[]{:S(2)}) collective-permute-start(bf16[256,1024]{0,1:T(8,128)(2,1)S(1)} %bitcast.58), channel_id=1, source_target_pairs={{0,7},{1,0},{2,1},{3,2},{4,3},{5,4},{6,5},{7,6},{8,15},{9,8},{10,9... | collective-permute-start | bytes 1572872 | tf_op jit(solution)/shard_map/ppermute | solution.py:154
  67.3 2.2 %collective-permute-start.2 = (bf16[1,256,512]{2,1,0:T(8,128)(2,1)}, bf16[1,256,512]{2,1,0:T(8,128)(2,1)S(1)}, u32[]{:S(2)}, u32[]{:S(2)}) collective-permute-start(bf16[1,256,512]{2,1,0:T(8,128)(2,1)} %get-tuple-element.29), channel_id=1, source_target_pairs={{2,0},{3,1},{6,4},{7,5},{10,8},{11,9},{14,12},{15,13},{18,16},{19,... | collective-permute-start | bytes 786440 | tf_op jit(solution)/shard_map/ppermute | solution.py:181
  69.5 2.9 %collective-permute-start.3 = (bf16[1,256,512]{2,1,0:T(8,128)(2,1)}, bf16[1,256,512]{2,1,0:T(8,128)(2,1)}, u32[]{:S(2)}, u32[]{:S(2)}) collective-permute-start(bf16[1,256,512]{2,1,0:T(8,128)(2,1)} %get-tuple-element.30), channel_id=1, source_target_pairs={{1,0},{2,1},{3,2},{5,4},{6,5},{7,6},{9,8},{10,9},{11,10},{13,12},{... | collective-permute-start | bytes 786440 | tf_op jit(solution)/shard_map/ppermute | solution.py:181
  72.4 0.1 constant_dynamic-update-slice_fusion.17
  72.6 0.1 constant_dynamic-update-slice_fusion.4
  72.7 2.9 %collective-permute-done.11 = bf16[256,1024]{0,1:T(8,128)(2,1)S(1)} collective-permute-done((bf16[256,1024]{0,1:T(8,128)(2,1)S(1)}, bf16[256,1024]{0,1:T(8,128)(2,1)S(1)}, u32[]{:S(2)}, u32[]{:S(2)}) %collective-permute-start.11) | collective-permute-done | bytes 524320 | tf_op jit(solution)/shard_map/ppermute | solution.py:154
  75.6 1.0 collective-permute-start.14
  76.7 12.2 %collective-permute-done.12 = bf16[256,1024]{0,1:T(8,128)(2,1)S(1)} collective-permute-done((bf16[256,1024]{0,1:T(8,128)(2,1)S(1)}, bf16[256,1024]{0,1:T(8,128)(2,1)S(1)}, u32[]{:S(2)}, u32[]{:S(2)}) %collective-permute-start.12) | collective-permute-done | bytes 524320 | tf_op jit(solution)/shard_map/ppermute | solution.py:154
  88.9 2.9 %collective-permute-start.15 = (bf16[256,512]{1,0:T(8,128)(2,1)S(1)}, bf16[256,512]{1,0:T(8,128)(2,1)S(1)}, u32[]{:S(2)}, u32[]{:S(2)}) collective-permute-start(bf16[256,512]{1,0:T(8,128)(2,1)S(1)} %bitcast.64), channel_id=1, source_target_pairs={{0,3},{1,4},{2,5},{3,6},{4,7},{5,0},{6,1},{7,2},{8,11},{9,12},{10,... | collective-permute-start | bytes 786440 | tf_op jit(solution)/shard_map/ppermute | solution.py:191
  92.0 0.3 collective-permute-start.16
  92.2 0.2 collective-permute-done.14
  92.5 9.9 %collective-permute-start.17 = (bf16[256,512]{1,0:T(8,128)(2,1)S(1)}, bf16[256,512]{1,0:T(8,128)(2,1)S(1)}, u32[]{:S(2)}, u32[]{:S(2)}) collective-permute-start(bf16[256,512]{1,0:T(8,128)(2,1)S(1)} %bitcast.66), channel_id=1, source_target_pairs={{0,5},{1,6},{2,7},{3,0},{4,1},{5,2},{6,3},{7,4},{8,13},{9,14},{10,... | collective-permute-start | bytes 786440 | tf_op jit(solution)/shard_map/ppermute | solution.py:191
  102.4 2.2 %collective-permute-start.18 = (bf16[256,512]{1,0:T(8,128)(2,1)S(1)}, bf16[256,512]{1,0:T(8,128)(2,1)S(1)}, u32[]{:S(2)}, u32[]{:S(2)}) collective-permute-start(bf16[256,512]{1,0:T(8,128)(2,1)S(1)} %bitcast.67), channel_id=1, source_target_pairs={{0,6},{1,7},{2,0},{3,1},{4,2},{5,3},{6,4},{7,5},{8,14},{9,15},{10,... | collective-permute-start | bytes 786440 | tf_op jit(solution)/shard_map/ppermute | solution.py:191
  104.6 1.7 %collective-permute-start.19 = (bf16[256,512]{1,0:T(8,128)(2,1)S(1)}, bf16[256,512]{1,0:T(8,128)(2,1)S(1)}, u32[]{:S(2)}, u32[]{:S(2)}) collective-permute-start(bf16[256,512]{1,0:T(8,128)(2,1)S(1)} %bitcast.68), channel_id=1, source_target_pairs={{0,7},{1,0},{2,1},{3,2},{4,3},{5,4},{6,5},{7,6},{8,15},{9,8},{10,9... | collective-permute-start | bytes 786440 | tf_op jit(solution)/shard_map/ppermute | solution.py:191
  106.3 9.3 %collective-permute-done.17 = bf16[256,512]{1,0:T(8,128)(2,1)S(1)} collective-permute-done((bf16[256,512]{1,0:T(8,128)(2,1)S(1)}, bf16[256,512]{1,0:T(8,128)(2,1)S(1)}, u32[]{:S(2)}, u32[]{:S(2)}) %collective-permute-start.17) | collective-permute-done | bytes 262176 | tf_op jit(solution)/shard_map/ppermute | solution.py:191
  115.7 2.3 %convolution_multiply_fusion = f32[1024,512]{1,0:T(8,128)S(1)} fusion(bf16[2048,1024]{0,1:T(8,128)(2,1)S(1)} %constant_dynamic-update-slice_fusion.2, bf16[2048,512]{1,0:T(8,128)(2,1)S(1)} %constant_dynamic-update-slice_fusion.10), kind=kOutput, calls=%fused_computation | convolution fusion | flops 2148007936 | bytes 8388608 | tf_op jit(solution)/shard_map/dot_general | solution.py:194
  118.1 0.1 convert_element_type.48
  118.2 0.8 dynamic-slice_bitcast_fusion.2
  119.0 1.3 collective-permute-start.20
  120.3 2.0 %collective-permute-start.22 = (bf16[256,512]{1,0:T(8,128)(2,1)S(1)}, bf16[256,512]{1,0:T(8,128)(2,1)}, u32[]{:S(2)}, u32[]{:S(2)}) collective-permute-start(bf16[256,512]{1,0:T(8,128)(2,1)S(1)} %get-tuple-element.25), channel_id=1, source_target_pairs={{0,24},{4,28},{8,0},{12,4},{16,8},{20,12},{24,16},{28,20},{1,25},{... | collective-permute-start | bytes 786440 | tf_op jit(solution)/shard_map/ppermute | solution.py:204
  122.3 0.4 collective-permute-start.21
  122.8 1.8 %fusion.5 = bf16[1,256,512]{2,1,0:T(8,128)(2,1)} fusion(f32[256,512]{1,0:T(8,128)S(1)} %get-tuple-element.10, bf16[1,256,512]{2,1,0:T(8,128)(2,1)} %collective-permute-done.3, bf16[1,256,512]{2,1,0:T(8,128)(2,1)S(1)} %collective-permute-done.2), kind=kLoop, calls=%fused_computation.10 | loop fusion | flops 655360 | bytes 1310720 | tf_op jit(solution)/shard_map/convert_element_type | solution.py:184
  124.5 4.9 %collective-permute-done.20 = bf16[256,512]{1,0:T(8,128)(2,1)} collective-permute-done((bf16[256,512]{1,0:T(8,128)(2,1)}, bf16[256,512]{1,0:T(8,128)(2,1)}, u32[]{:S(2)}, u32[]{:S(2)}) %collective-permute-start.20) | collective-permute-done | bytes 262176 | tf_op jit(solution)/shard_map/ppermute | solution.py:204
  129.4 4.5 %collective-permute-done.22 = bf16[256,512]{1,0:T(8,128)(2,1)} collective-permute-done((bf16[256,512]{1,0:T(8,128)(2,1)S(1)}, bf16[256,512]{1,0:T(8,128)(2,1)}, u32[]{:S(2)}, u32[]{:S(2)}) %collective-permute-start.22) | collective-permute-done | bytes 262176 | tf_op jit(solution)/shard_map/ppermute | solution.py:204
  133.9 12.4 %collective-permute-done.21 = bf16[256,512]{1,0:T(8,128)(2,1)} collective-permute-done((bf16[256,512]{1,0:T(8,128)(2,1)S(1)}, bf16[256,512]{1,0:T(8,128)(2,1)}, u32[]{:S(2)}, u32[]{:S(2)}) %collective-permute-start.21) | collective-permute-done | bytes 262176 | tf_op jit(solution)/shard_map/ppermute | solution.py:204
  146.3 2.0 %fusion.1 = f32[256,512]{1,0:T(8,128)} fusion(bf16[256,512]{1,0:T(8,128)(2,1)} %collective-permute-done.22, bf16[256,512]{1,0:T(8,128)(2,1)} %collective-permute-done.21, bf16[256,512]{1,0:T(8,128)(2,1)} %collective-permute-done.20, f32[4,256,512]{2,1,0:T(8,128)S(1)} %bitcast.56, s32[]{:T(128)S(6)} %select_n.69), kind=kLoop, calls=%fused_computation.4 | loop fusion | flops 786432 | bytes 1835012 | tf_op jit(solution)/shard_map/add | solution.py:204
  (44 shorter events, 0.6 us)
Async XLA Ops:
  2.6 19.1 %collective-permute-start.1 = (bf16[1,256,1024]{2,1,0:T(8,128)(2,1)S(1)}, bf16[1,256,1024]{2,1,0:T(8,128)(2,1)S(1)}, u32[]{:S(2)}, u32[]{:S(2)}) collective-permute-start(bf16[1,256,1024]{2,1,0:T(8,128)(2,1)S(1)} %constant_dynamic-update-slice_fusion), channel_id=1, source_target_pairs={{0,1},{1,2},{2,3},{4,5},{5,6},{6,7},{8,9},{9,10},{10,11},{12,13},{... | collective-permute-start | bytes 1572872 | tf_op jit(solution)/shard_map/ppermute | solution.py:131
  3.9 20.5 %collective-permute-start = (bf16[1,256,1024]{2,1,0:T(8,128)(2,1)S(1)}, bf16[1,256,1024]{2,1,0:T(8,128)(2,1)}, u32[]{:S(2)}, u32[]{:S(2)}) collective-permute-start(bf16[1,256,1024]{2,1,0:T(8,128)(2,1)S(1)} %constant_dynamic-update-slice_fusion), channel_id=1, source_target_pairs={{0,2},{1,3},{4,6},{5,7},{8,10},{9,11},{12,14},{13,15},{16,18},{17,... | collective-permute-start | bytes 1572872 | tf_op jit(solution)/shard_map/ppermute | solution.py:131
  11.6 9.6 %copy-start.5 = (s32[1,8]{1,0:T(1,128)S(1)}, s32[1,8]{1,0:T(1,128)}, u32[]{:S(2)}) copy-start(s32[1,8]{1,0:T(1,128)} %param.11) | copy-start | bytes 100
  15.7 56.9 %collective-permute-start.10 = (bf16[256,1024]{0,1:T(8,128)(2,1)}, bf16[256,1024]{0,1:T(8,128)(2,1)S(1)}, u32[]{:S(2)}, u32[]{:S(2)}) collective-permute-start(bf16[256,1024]{0,1:T(8,128)(2,1)} %bitcast.17), channel_id=1, source_target_pairs={{0,5},{1,6},{2,7},{3,0},{4,1},{5,2},{6,3},{7,4},{8,13},{9,14},{10,... | collective-permute-start | bytes 1572872 | tf_op jit(solution)/shard_map/ppermute | solution.py:154
  19.9 45.7 %collective-permute-start.9 = (bf16[256,1024]{0,1:T(8,128)(2,1)}, bf16[256,1024]{0,1:T(8,128)(2,1)S(1)}, u32[]{:S(2)}, u32[]{:S(2)}) collective-permute-start(bf16[256,1024]{0,1:T(8,128)(2,1)} %bitcast.16), channel_id=1, source_target_pairs={{0,4},{1,5},{2,6},{3,7},{4,0},{5,1},{6,2},{7,3},{8,12},{9,13},{10,... | collective-permute-start | bytes 1572872 | tf_op jit(solution)/shard_map/ppermute | solution.py:154
  21.2 37.4 %collective-permute-start.8 = (bf16[256,1024]{0,1:T(8,128)(2,1)}, bf16[256,1024]{0,1:T(8,128)(2,1)S(1)}, u32[]{:S(2)}, u32[]{:S(2)}) collective-permute-start(bf16[256,1024]{0,1:T(8,128)(2,1)} %bitcast.15), channel_id=1, source_target_pairs={{0,3},{1,4},{2,5},{3,6},{4,7},{5,0},{6,1},{7,2},{8,11},{9,12},{10,... | collective-permute-start | bytes 1572872 | tf_op jit(solution)/shard_map/ppermute | solution.py:154
  21.6 3.9 %copy-start = (bf16[1,256,4096]{2,1,0:T(8,128)(2,1)S(1)}, bf16[1,256,4096]{2,1,0:T(8,128)(2,1)}, u32[]{:S(2)}) copy-start(bf16[1,256,4096]{2,1,0:T(8,128)(2,1)} %param.6) | copy-start | bytes 6291460
  21.7 3.9 %copy-start.1 = (bf16[1,256,4096]{2,1,0:T(8,128)(2,1)S(1)}, bf16[1,256,4096]{2,1,0:T(8,128)(2,1)}, u32[]{:S(2)}) copy-start(bf16[1,256,4096]{2,1,0:T(8,128)(2,1)} %param.9) | copy-start | bytes 6291460
  21.7 35.0 %collective-permute-start.7 = (bf16[256,1024]{0,1:T(8,128)(2,1)}, bf16[256,1024]{0,1:T(8,128)(2,1)S(1)}, u32[]{:S(2)}, u32[]{:S(2)}) collective-permute-start(bf16[256,1024]{0,1:T(8,128)(2,1)} %bitcast.60), channel_id=1, source_target_pairs={{0,2},{1,3},{2,4},{3,5},{4,6},{5,7},{6,0},{7,1},{8,10},{9,11},{10,... | collective-permute-start | bytes 1572872 | tf_op jit(solution)/shard_map/ppermute | solution.py:154
  24.4 28.5 %collective-permute-start.6 = (bf16[256,1024]{0,1:T(8,128)(2,1)}, bf16[256,1024]{0,1:T(8,128)(2,1)S(1)}, u32[]{:S(2)}, u32[]{:S(2)}) collective-permute-start(bf16[256,1024]{0,1:T(8,128)(2,1)} %bitcast.61), channel_id=1, source_target_pairs={{0,1},{1,2},{2,3},{3,4},{4,5},{5,6},{6,7},{7,0},{8,9},{9,10},{10,1... | collective-permute-start | bytes 1572872 | tf_op jit(solution)/shard_map/ppermute | solution.py:154
  52.9 5.6 %copy-start.3 = (bf16[256,4,1,256]{0,3,2,1:T(8,128)(2,1)S(1)}, bf16[256,4,1,256]{0,3,2,1:T(8,128)(2,1)}, u32[]{:S(2)}) copy-start(bf16[256,4,1,256]{0,3,2,1:T(8,128)(2,1)} %get-tuple-element.17) | copy-start | bytes 1572868
  53.0 12.7 %copy-start.2 = (bf16[256,4,1,256]{0,3,2,1:T(8,128)(2,1)S(1)}, bf16[256,4,1,256]{0,3,2,1:T(8,128)(2,1)}, u32[]{:S(2)}) copy-start(bf16[256,4,1,256]{0,3,2,1:T(8,128)(2,1)} %get-tuple-element.16) | copy-start | bytes 1572868
  53.0 14.3 %collective-permute-start.4 = (bf16[1,256,512]{2,1,0:T(8,128)(2,1)S(1)}, bf16[1,256,512]{2,1,0:T(8,128)(2,1)S(1)}, u32[]{:S(2)}, u32[]{:S(2)}) collective-permute-start(bf16[1,256,512]{2,1,0:T(8,128)(2,1)S(1)} %get-tuple-element.27), channel_id=1, source_target_pairs={{2,0},{3,1},{6,4},{7,5},{10,8},{11,9},{14,12},{15,13},{18,16},{19,... | collective-permute-start | bytes 786440 | tf_op jit(solution)/shard_map/ppermute | solution.py:181
  56.7 12.8 %collective-permute-start.5 = (bf16[1,256,512]{2,1,0:T(8,128)(2,1)S(1)}, bf16[1,256,512]{2,1,0:T(8,128)(2,1)S(1)}, u32[]{:S(2)}, u32[]{:S(2)}) collective-permute-start(bf16[1,256,512]{2,1,0:T(8,128)(2,1)S(1)} %get-tuple-element.28), channel_id=1, source_target_pairs={{1,0},{2,1},{3,2},{5,4},{6,5},{7,6},{9,8},{10,9},{11,10},{13,12},{... | collective-permute-start | bytes 786440 | tf_op jit(solution)/shard_map/ppermute | solution.py:181
  58.6 17.0 %collective-permute-start.11 = (bf16[256,1024]{0,1:T(8,128)(2,1)S(1)}, bf16[256,1024]{0,1:T(8,128)(2,1)S(1)}, u32[]{:S(2)}, u32[]{:S(2)}) collective-permute-start(bf16[256,1024]{0,1:T(8,128)(2,1)S(1)} %bitcast.59), channel_id=1, source_target_pairs={{0,6},{1,7},{2,0},{3,1},{4,2},{5,3},{6,4},{7,5},{8,14},{9,15},{10,... | collective-permute-start | bytes 1572872 | tf_op jit(solution)/shard_map/ppermute | solution.py:154
  65.7 23.3 %collective-permute-start.12 = (bf16[256,1024]{0,1:T(8,128)(2,1)S(1)}, bf16[256,1024]{0,1:T(8,128)(2,1)S(1)}, u32[]{:S(2)}, u32[]{:S(2)}) collective-permute-start(bf16[256,1024]{0,1:T(8,128)(2,1)S(1)} %bitcast.58), channel_id=1, source_target_pairs={{0,7},{1,0},{2,1},{3,2},{4,3},{5,4},{6,5},{7,6},{8,15},{9,8},{10,9... | collective-permute-start | bytes 1572872 | tf_op jit(solution)/shard_map/ppermute | solution.py:154
  67.3 55.4 %collective-permute-start.2 = (bf16[1,256,512]{2,1,0:T(8,128)(2,1)}, bf16[1,256,512]{2,1,0:T(8,128)(2,1)S(1)}, u32[]{:S(2)}, u32[]{:S(2)}) collective-permute-start(bf16[1,256,512]{2,1,0:T(8,128)(2,1)} %get-tuple-element.29), channel_id=1, source_target_pairs={{2,0},{3,1},{6,4},{7,5},{10,8},{11,9},{14,12},{15,13},{18,16},{19,... | collective-permute-start | bytes 786440 | tf_op jit(solution)/shard_map/ppermute | solution.py:181
  69.5 53.2 %collective-permute-start.3 = (bf16[1,256,512]{2,1,0:T(8,128)(2,1)}, bf16[1,256,512]{2,1,0:T(8,128)(2,1)}, u32[]{:S(2)}, u32[]{:S(2)}) collective-permute-start(bf16[1,256,512]{2,1,0:T(8,128)(2,1)} %get-tuple-element.30), channel_id=1, source_target_pairs={{1,0},{2,1},{3,2},{5,4},{6,5},{7,6},{9,8},{10,9},{11,10},{13,12},{... | collective-permute-start | bytes 786440 | tf_op jit(solution)/shard_map/ppermute | solution.py:181
  72.6 32.0 %copy-start.4 = (bf16[1,256,512]{2,1,0:T(8,128)(2,1)}, bf16[1,256,512]{2,1,0:T(8,128)(2,1)S(1)}, u32[]{:S(2)}) copy-start(bf16[1,256,512]{2,1,0:T(8,128)(2,1)S(1)} %get-tuple-element.15) | copy-start | bytes 786436
  72.6 19.4 %collective-permute-start.13 = (bf16[256,512]{1,0:T(8,128)(2,1)S(1)}, bf16[256,512]{1,0:T(8,128)(2,1)S(1)}, u32[]{:S(2)}, u32[]{:S(2)}) collective-permute-start(bf16[256,512]{1,0:T(8,128)(2,1)S(1)} %bitcast.62), channel_id=1, source_target_pairs={{0,1},{1,2},{2,3},{3,4},{4,5},{5,6},{6,7},{7,0},{8,9},{9,10},{10,1... | collective-permute-start | bytes 786440 | tf_op jit(solution)/shard_map/ppermute | solution.py:191
  75.6 16.9 %collective-permute-start.14 = (bf16[256,512]{1,0:T(8,128)(2,1)S(1)}, bf16[256,512]{1,0:T(8,128)(2,1)S(1)}, u32[]{:S(2)}, u32[]{:S(2)}) collective-permute-start(bf16[256,512]{1,0:T(8,128)(2,1)S(1)} %bitcast.63), channel_id=1, source_target_pairs={{0,2},{1,3},{2,4},{3,5},{4,6},{5,7},{6,0},{7,1},{8,10},{9,11},{10,... | collective-permute-start | bytes 786440 | tf_op jit(solution)/shard_map/ppermute | solution.py:191
  88.9 13.4 %collective-permute-start.15 = (bf16[256,512]{1,0:T(8,128)(2,1)S(1)}, bf16[256,512]{1,0:T(8,128)(2,1)S(1)}, u32[]{:S(2)}, u32[]{:S(2)}) collective-permute-start(bf16[256,512]{1,0:T(8,128)(2,1)S(1)} %bitcast.64), channel_id=1, source_target_pairs={{0,3},{1,4},{2,5},{3,6},{4,7},{5,0},{6,1},{7,2},{8,11},{9,12},{10,... | collective-permute-start | bytes 786440 | tf_op jit(solution)/shard_map/ppermute | solution.py:191
  92.0 12.6 %collective-permute-start.16 = (bf16[256,512]{1,0:T(8,128)(2,1)S(1)}, bf16[256,512]{1,0:T(8,128)(2,1)S(1)}, u32[]{:S(2)}, u32[]{:S(2)}) collective-permute-start(bf16[256,512]{1,0:T(8,128)(2,1)S(1)} %bitcast.65), channel_id=1, source_target_pairs={{0,4},{1,5},{2,6},{3,7},{4,0},{5,1},{6,2},{7,3},{8,12},{9,13},{10,... | collective-permute-start | bytes 786440 | tf_op jit(solution)/shard_map/ppermute | solution.py:191
  92.5 23.2 %collective-permute-start.17 = (bf16[256,512]{1,0:T(8,128)(2,1)S(1)}, bf16[256,512]{1,0:T(8,128)(2,1)S(1)}, u32[]{:S(2)}, u32[]{:S(2)}) collective-permute-start(bf16[256,512]{1,0:T(8,128)(2,1)S(1)} %bitcast.66), channel_id=1, source_target_pairs={{0,5},{1,6},{2,7},{3,0},{4,1},{5,2},{6,3},{7,4},{8,13},{9,14},{10,... | collective-permute-start | bytes 786440 | tf_op jit(solution)/shard_map/ppermute | solution.py:191
  102.4 13.3 %collective-permute-start.18 = (bf16[256,512]{1,0:T(8,128)(2,1)S(1)}, bf16[256,512]{1,0:T(8,128)(2,1)S(1)}, u32[]{:S(2)}, u32[]{:S(2)}) collective-permute-start(bf16[256,512]{1,0:T(8,128)(2,1)S(1)} %bitcast.67), channel_id=1, source_target_pairs={{0,6},{1,7},{2,0},{3,1},{4,2},{5,3},{6,4},{7,5},{8,14},{9,15},{10,... | collective-permute-start | bytes 786440 | tf_op jit(solution)/shard_map/ppermute | solution.py:191
  104.6 11.1 %collective-permute-start.19 = (bf16[256,512]{1,0:T(8,128)(2,1)S(1)}, bf16[256,512]{1,0:T(8,128)(2,1)S(1)}, u32[]{:S(2)}, u32[]{:S(2)}) collective-permute-start(bf16[256,512]{1,0:T(8,128)(2,1)S(1)} %bitcast.68), channel_id=1, source_target_pairs={{0,7},{1,0},{2,1},{3,2},{4,3},{5,4},{6,5},{7,6},{8,15},{9,8},{10,9... | collective-permute-start | bytes 786440 | tf_op jit(solution)/shard_map/ppermute | solution.py:191
  119.0 10.4 %collective-permute-start.20 = (bf16[256,512]{1,0:T(8,128)(2,1)}, bf16[256,512]{1,0:T(8,128)(2,1)}, u32[]{:S(2)}, u32[]{:S(2)}) collective-permute-start(bf16[256,512]{1,0:T(8,128)(2,1)} %get-tuple-element.24), channel_id=1, source_target_pairs={{0,8},{4,12},{8,16},{12,20},{16,24},{20,28},{24,0},{28,4},{1,9},{5... | collective-permute-start | bytes 786440 | tf_op jit(solution)/shard_map/ppermute | solution.py:204
  120.3 13.6 %collective-permute-start.22 = (bf16[256,512]{1,0:T(8,128)(2,1)S(1)}, bf16[256,512]{1,0:T(8,128)(2,1)}, u32[]{:S(2)}, u32[]{:S(2)}) collective-permute-start(bf16[256,512]{1,0:T(8,128)(2,1)S(1)} %get-tuple-element.25), channel_id=1, source_target_pairs={{0,24},{4,28},{8,0},{12,4},{16,8},{20,12},{24,16},{28,20},{1,25},{... | collective-permute-start | bytes 786440 | tf_op jit(solution)/shard_map/ppermute | solution.py:204
  122.3 24.0 %collective-permute-start.21 = (bf16[256,512]{1,0:T(8,128)(2,1)S(1)}, bf16[256,512]{1,0:T(8,128)(2,1)}, u32[]{:S(2)}, u32[]{:S(2)}) collective-permute-start(bf16[256,512]{1,0:T(8,128)(2,1)S(1)} %get-tuple-element.26), channel_id=1, source_target_pairs={{0,16},{4,20},{8,24},{12,28},{16,0},{20,4},{24,8},{28,12},{1,17},{... | collective-permute-start | bytes 786440 | tf_op jit(solution)/shard_map/ppermute | solution.py:204

commit v2 on v1

--- a/solution.py
+++ b/solution.py
@@ -144,15 +144,17 @@
         block = lax.dynamic_slice_in_dim(split_input, owner, 1, axis=2)
         return block.reshape(streams * local_len, groups * piece)
 
-    def ring(s):
+    def flip(t):
         return [
-            (z * members + i, z * members + (i + s) % members)
-            for z in range(groups) for i in range(members)
+            (z * members + i, z * members + (i ^ t)) for z in range(groups) for i in range(members)
         ]
 
+    order, bit = [0], members // 2
+    while bit:
+        order = order + [t ^ bit for t in order]
+        bit //= 2
     inputs = [columns_of(member)] + [
-        lax.ppermute(columns_of(lax.rem(member + s, members)), both, ring(s))
-        for s in range(1, members)
+        lax.ppermute(columns_of(jnp.bitwise_xor(member, t)), both, flip(t)) for t in order[1:]
     ]
     all_inputs = jnp.concatenate(inputs, axis=0)
 
@@ -187,10 +189,11 @@
     key_grad = collect(key_own, key_prior)
 
     flat_value = value_grad.reshape(streams * local_len, kv_width)
-    all_values = jnp.concatenate(
-        [flat_value] + [lax.ppermute(flat_value, both, ring(s)) for s in range(1, members)],
-        axis=0,
-    )
+    all_values, bit = flat_value, members // 2
+    while bit:
+        received = lax.ppermute(all_values, both, flip(bit))
+        all_values = jnp.concatenate([all_values, received], axis=0)
+        bit //= 2
     partial = lax.dot_general(
         all_inputs, all_values, (((0,), (0,)), ((), ())), preferred_element_type=jnp.float32
     ) / math.sqrt(streams * dp_count * full_len)

time: 149 us -> 167 us (1.12)
  the two profiles are of different devices: /device:TPU:3 before, /device:TPU:15 now
where the time goes in v2:
time: 167 us; the launch traced here: 166 us
  waiting for transfers between devices  65.4 us (39%)
  starting transfers between devices  36.7 us (22%)
  Pallas kernels  27.3 us (16%)
  local copies, waits for them, and re-layouts  23.3 us (14%)
  other arithmetic  8.12 us (5%)
  matrix products  4.63 us (3%)
    pallas_call x1, Pallas kernels, attention_grads(): pl.pallas_call(functools.partial(attention_kernel, prior, group), grid=(k...  27.3 us
    ppermute x7, waiting for transfers between devices, shards(): lax.ppermute(columns_of(jnp.bitwise_xor(member, t)), both, flip(t))  26.6 us
    ppermute x3, waiting for transfers between devices, shards(): lax.ppermute(block, 'dp', turn).astype(jnp.float32)  20.5 us
    ppermute x4, starting transfers between devices, collect(): lax.ppermute(block, 'seq', [(i + s, i) for i in range(seq_count - s)])  17.2 us
    unnamed x21, local copies, waits for them, and re-layouts  16.2 us
    ppermute x2, waiting for transfers between devices, shards(): lax.ppermute(own_kv, 'seq', [(i, i + s) for i in range(seq_count - s)])  11 us
    ppermute x7, starting transfers between devices, shards(): lax.ppermute(columns_of(jnp.bitwise_xor(member, t)), both, flip(t))  7.34 us
    ppermute x3, starting transfers between devices, shards(): received = lax.ppermute(all_values, both, flip(bit))  5.77 us
  transfers between devices with their start and end apart: 19, of which 11 were waited for; matrix products, arithmetic and copies ran while one was open for 17% of the time, Pallas kernels for 0%

profile of v2, /device:TPU:15, one launch (start us, length us, event | category | flops | bytes accessed | tf_op | source)
XLA Modules:
  0.0 166.2 jit_solution(5755124627683905945)
XLA Ops:
  0.6 1.1 constant_dynamic-update-slice_fusion.1
  1.8 1.0 constant_dynamic-update-slice_fusion
  2.8 1.3 collective-permute-start
  4.1 1.3 collective-permute-start.1
  5.4 0.8 select_reduce_fusion
  6.5 11.0 %collective-permute-done = bf16[1,256,1024]{2,1,0:T(8,128)(2,1)S(1)} collective-permute-done((bf16[1,256,1024]{2,1,0:T(8,128)(2,1)S(1)}, bf16[1,256,1024]{2,1,0:T(8,128)(2,1)S(1)}, u32[]{:S(2)}, u32[]{:S(2)}) %collective-permute-start) | collective-permute-done | bytes 524320 | tf_op jit(solution)/shard_map/ppermute | solution.py:131
  17.4 1.2 maximum_bitcast_fusion.k_ref.v_ref
  18.6 1.6 copy-done.1
  20.2 27.3 %shard_map.93 = (bf16[256,4096]{1,0:T(8,128)(2,1)}, bf16[512,512]{1,0:T(8,128)(2,1)S(1)}, bf16[512,512]{1,0:T(8,128)(2,1)S(1)}, f32[256,512]{1,0:T(8,128)S(1)}, f32[256,512]{1,0:T(8,128)S(1)}) custom-call(bf16[256,4096]{1,0:T(8,128)(2,1)S(1)} %bitcast.49, bf16[256,4096]{1,0:T(8,128)(2,1)S(1)} %bitcast.50, ...), custom_call_target="tpu_custom_call" | custom-call | flops 8053063680 | bytes 10485760 | tf_op jit(solution)/shard_map/pallas_call | solution.py:80
  47.5 8.0 %collective-permute-start.4 = (bf16[1,256,512]{2,1,0:T(8,128)(2,1)S(1)}, bf16[1,256,512]{2,1,0:T(8,128)(2,1)S(1)}, u32[]{:S(2)}, u32[]{:S(2)}) collective-permute-start(bf16[1,256,512]{2,1,0:T(8,128)(2,1)S(1)} %get-tuple-element.25), channel_id=1, source_target_pairs={{2,0},{3,1},{6,4},{7,5},{10,8},{11,9},{14,12},{15,13},{18,16},{19,... | collective-permute-start | bytes 786440 | tf_op jit(solution)/shard_map/ppermute | solution.py:183
  55.5 2.5 %collective-permute-start.5 = (bf16[1,256,512]{2,1,0:T(8,128)(2,1)S(1)}, bf16[1,256,512]{2,1,0:T(8,128)(2,1)S(1)}, u32[]{:S(2)}, u32[]{:S(2)}) collective-permute-start(bf16[1,256,512]{2,1,0:T(8,128)(2,1)S(1)} %get-tuple-element.26), channel_id=1, source_target_pairs={{1,0},{2,1},{3,2},{5,4},{6,5},{7,6},{9,8},{10,9},{11,10},{13,12},{... | collective-permute-start | bytes 786440 | tf_op jit(solution)/shard_map/ppermute | solution.py:183
  58.0 2.8 %collective-permute-done.4 = bf16[1,256,512]{2,1,0:T(8,128)(2,1)S(1)} collective-permute-done((bf16[1,256,512]{2,1,0:T(8,128)(2,1)S(1)}, bf16[1,256,512]{2,1,0:T(8,128)(2,1)S(1)}, u32[]{:S(2)}, u32[]{:S(2)}) %collective-permute-start.4) | collective-permute-done | bytes 262176 | tf_op jit(solution)/shard_map/ppermute | solution.py:183
  61.2 6.4 %copy.14 = bf16[1,256,8192]{1,2,0:T(8,128)(2,1)} copy(bf16[1,256,8192]{2,1,0:T(8,128)(2,1)} %param.10) | data formatting | bytes 8388608 | tf_op args[4]
  67.6 0.9 pad_maximum_fusion.1
  68.5 5.5 %collective-permute-start.14 = (bf16[512,512]{1,0:T(8,128)(2,1)}, bf16[512,512]{1,0:T(8,128)(2,1)}, u32[]{:S(2)}, u32[]{:S(2)}) collective-permute-start(bf16[512,512]{1,0:T(8,128)(2,1)} %pad_maximum_fusion.1), channel_id=1, source_target_pairs={{0,2},{1,3},{2,0},{3,1},{4,6},{5,7},{6,4},{7,5},{8,10},{9,11},{10,... | collective-permute-start | bytes 1572872 | tf_op jit(solution)/shard_map/ppermute | solution.py:194
  74.0 4.1 %constant_dynamic-slice_fusion = (bf16[256,4,1,256]{0,3,2,1:T(8,128)(2,1)}, bf16[256,4,1,256]{0,3,2,1:T(8,128)(2,1)}, bf16[256,4,1,256]{0,3,2,1:T(8,128)(2,1)}, ...) fusion(bf16[256,4,8,256]{0,3,2,1:T(8,128)(2,1)} %bitcast.51, ...), kind=kLoop, calls=%fused_computation.40 | loop fusion | bytes 8388640 | tf_op jit(solution)/shard_map/dynamic_slice | solution.py:144
  78.0 1.2 collective-permute-start.6
  79.3 1.4 collective-permute-start.8
  80.7 0.9 constant_dynamic-update-slice_fusion.9
  81.5 4.6 %collective-permute-done.14 = bf16[512,512]{1,0:T(8,128)(2,1)} collective-permute-done((bf16[512,512]{1,0:T(8,128)(2,1)}, bf16[512,512]{1,0:T(8,128)(2,1)}, u32[]{:S(2)}, u32[]{:S(2)}) %collective-permute-start.14) | collective-permute-done | bytes 524320 | tf_op jit(solution)/shard_map/ppermute | solution.py:194
  86.1 2.8 %collective-permute-start.10 = (bf16[256,1024]{0,1:T(8,128)(2,1)}, bf16[256,1024]{0,1:T(8,128)(2,1)S(1)}, u32[]{:S(2)}, u32[]{:S(2)}) collective-permute-start(bf16[256,1024]{0,1:T(8,128)(2,1)} %bitcast.61), channel_id=1, source_target_pairs={{0,5},{1,4},{2,7},{3,6},{4,1},{5,0},{6,3},{7,2},{8,13},{9,12},{10,... | collective-permute-start | bytes 1572872 | tf_op jit(solution)/shard_map/ppermute | solution.py:157
  88.9 1.1 pad_maximum_fusion
  90.0 2.1 %collective-permute-done.6 = bf16[256,1024]{0,1:T(8,128)(2,1)} collective-permute-done((bf16[256,1024]{0,1:T(8,128)(2,1)}, bf16[256,1024]{0,1:T(8,128)(2,1)}, u32[]{:S(2)}, u32[]{:S(2)}) %collective-permute-start.6) | collective-permute-done | bytes 524320 | tf_op jit(solution)/shard_map/ppermute | solution.py:157
  92.1 0.8 fusion.20
  92.9 4.3 %collective-permute-done.7 = bf16[256,1024]{0,1:T(8,128)(2,1)S(1)} collective-permute-done((bf16[256,1024]{0,1:T(8,128)(2,1)}, bf16[256,1024]{0,1:T(8,128)(2,1)S(1)}, u32[]{:S(2)}, u32[]{:S(2)}) %collective-permute-start.7) | collective-permute-done | bytes 524320 | tf_op jit(solution)/shard_map/ppermute | solution.py:157
  97.2 0.9 collective-permute-start.11
  98.2 1.9 %constant_dynamic-update-slice_fusion.8 = bf16[2048,1024]{0,1:T(8,128)(2,1)} fusion(bf16[2048,1024]{0,1:T(8,128)(2,1)} %constant_dynamic-update-slice_fusion.9, bf16[256,1024]{0,1:T(8,128)(2,1)} %collective-permute-done.6), kind=kLoop, calls=%fused_computation.34 | loop fusion | bytes 1048576
  100.1 9.4 %collective-permute-done.8 = bf16[256,1024]{0,1:T(8,128)(2,1)S(1)} collective-permute-done((bf16[256,1024]{0,1:T(8,128)(2,1)}, bf16[256,1024]{0,1:T(8,128)(2,1)S(1)}, u32[]{:S(2)}, u32[]{:S(2)}) %collective-permute-start.8) | collective-permute-done | bytes 524320 | tf_op jit(solution)/shard_map/ppermute | solution.py:157
  109.5 0.9 collective-permute-start.12
  110.4 0.9 constant_dynamic-update-slice_fusion.7
  111.3 0.9 constant_dynamic-update-slice_fusion.6
  112.2 4.6 %collective-permute-start.2 = (bf16[1,256,512]{2,1,0:T(8,128)(2,1)}, bf16[1,256,512]{2,1,0:T(8,128)(2,1)}, u32[]{:S(2)}, u32[]{:S(2)}) collective-permute-start(bf16[1,256,512]{2,1,0:T(8,128)(2,1)} %get-tuple-element.27), channel_id=1, source_target_pairs={{2,0},{3,1},{6,4},{7,5},{10,8},{11,9},{14,12},{15,13},{18,16},{19,... | collective-permute-start | bytes 786440 | tf_op jit(solution)/shard_map/ppermute | solution.py:183
  116.8 0.9 constant_dynamic-update-slice_fusion.5
  117.7 2.1 %collective-permute-start.3 = (bf16[1,256,512]{2,1,0:T(8,128)(2,1)}, bf16[1,256,512]{2,1,0:T(8,128)(2,1)}, u32[]{:S(2)}, u32[]{:S(2)}) collective-permute-start(bf16[1,256,512]{2,1,0:T(8,128)(2,1)} %get-tuple-element.28), channel_id=1, source_target_pairs={{1,0},{2,1},{3,2},{5,4},{6,5},{7,6},{9,8},{10,9},{11,10},{13,12},{... | collective-permute-start | bytes 786440 | tf_op jit(solution)/shard_map/ppermute | solution.py:183
  119.8 0.9 constant_dynamic-update-slice_fusion.4
  120.6 0.4 collective-permute-done.11
  121.0 0.8 constant_dynamic-update-slice_fusion.3
  121.9 10.4 %collective-permute-done.12 = bf16[256,1024]{0,1:T(8,128)(2,1)S(1)} collective-permute-done((bf16[256,1024]{0,1:T(8,128)(2,1)S(1)}, bf16[256,1024]{0,1:T(8,128)(2,1)S(1)}, u32[]{:S(2)}, u32[]{:S(2)}) %collective-permute-start.12) | collective-permute-done | bytes 524320 | tf_op jit(solution)/shard_map/ppermute | solution.py:157
  132.3 0.9 constant_dynamic-update-slice_fusion.2
  133.2 4.6 %fusion.8 = f32[1024,512]{1,0:T(8,128)S(1)} fusion(bf16[2048,1024]{0,1:T(8,128)(2,1)} %constant_dynamic-update-slice_fusion.2, bf16[1024,512]{1,0:T(8,128)(2,1)S(1)} %collective-permute-done.15, bf16[512,512]{1,0:T(8,128)(2,1)} %collective-permute-done.14, bf16[256,512]{1,0:T(8,128)(2,1)S(1)} %copy-done.4, bf16[256,512]{1,0:T(8,128)(2,1)S(1)} %bitcast.57), kind=kOutput, calls=%fused_computation.8 | convolution fusion | flops 2156396544 | bytes 8388608 | tf_op jit(solution)/shard_map/dot_general | solution.py:197
  138.0 1.4 collective-permute-start.16
  139.4 1.1 collective-permute-start.17
  140.5 1.4 collective-permute-start.18
  141.9 1.8 %fusion.16 = bf16[1,256,512]{2,1,0:T(8,128)(2,1)} fusion(f32[256,512]{1,0:T(8,128)S(1)} %get-tuple-element.10, bf16[1,256,512]{2,1,0:T(8,128)(2,1)} %collective-permute-done.3, bf16[1,256,512]{2,1,0:T(8,128)(2,1)} %collective-permute-done.2), kind=kLoop, calls=%fused_computation.20 | loop fusion | flops 655360 | bytes 1310720 | tf_op jit(solution)/shard_map/convert_element_type | solution.py:186
  143.7 2.4 %collective-permute-done.16 = bf16[256,512]{1,0:T(8,128)(2,1)} collective-permute-done((bf16[256,512]{1,0:T(8,128)(2,1)S(1)}, bf16[256,512]{1,0:T(8,128)(2,1)}, u32[]{:S(2)}, u32[]{:S(2)}) %collective-permute-start.16) | collective-permute-done | bytes 262176 | tf_op jit(solution)/shard_map/ppermute | solution.py:207
  146.1 15.8 %collective-permute-done.17 = bf16[256,512]{1,0:T(8,128)(2,1)} collective-permute-done((bf16[256,512]{1,0:T(8,128)(2,1)S(1)}, bf16[256,512]{1,0:T(8,128)(2,1)}, u32[]{:S(2)}, u32[]{:S(2)}) %collective-permute-start.17) | collective-permute-done | bytes 262176 | tf_op jit(solution)/shard_map/ppermute | solution.py:207
  161.9 2.3 %collective-permute-done.18 = bf16[256,512]{1,0:T(8,128)(2,1)} collective-permute-done((bf16[256,512]{1,0:T(8,128)(2,1)S(1)}, bf16[256,512]{1,0:T(8,128)(2,1)}, u32[]{:S(2)}, u32[]{:S(2)}) %collective-permute-start.18) | collective-permute-done | bytes 262176 | tf_op jit(solution)/shard_map/ppermute | solution.py:207
  164.2 2.0 %fusion.12 = f32[256,512]{1,0:T(8,128)} fusion(bf16[256,512]{1,0:T(8,128)(2,1)} %collective-permute-done.18, bf16[256,512]{1,0:T(8,128)(2,1)} %collective-permute-done.17, bf16[256,512]{1,0:T(8,128)(2,1)} %collective-permute-done.16, f32[4,256,512]{2,1,0:T(8,128)S(1)} %bitcast.53, s32[]{:T(128)S(6)} %select_n.69), kind=kLoop, calls=%fused_computation.14 | loop fusion | flops 786432 | bytes 1835012 | tf_op jit(solution)/shard_map/add | solution.py:207
  (31 shorter events, 1.0 us)
Async XLA Ops:
  0.6 18.0 %copy-start = (bf16[1,256,4096]{2,1,0:T(8,128)(2,1)S(1)}, bf16[1,256,4096]{2,1,0:T(8,128)(2,1)}, u32[]{:S(2)}) copy-start(bf16[1,256,4096]{2,1,0:T(8,128)(2,1)} %param.6) | copy-start | bytes 6291460
  2.8 14.7 %collective-permute-start = (bf16[1,256,1024]{2,1,0:T(8,128)(2,1)S(1)}, bf16[1,256,1024]{2,1,0:T(8,128)(2,1)S(1)}, u32[]{:S(2)}, u32[]{:S(2)}) collective-permute-start(bf16[1,256,1024]{2,1,0:T(8,128)(2,1)S(1)} %constant_dynamic-update-slice_fusion), channel_id=1, source_target_pairs={{0,2},{1,3},{4,6},{5,7},{8,10},{9,11},{12,14},{13,15},{16,18},{17,... | collective-permute-start | bytes 1572872 | tf_op jit(solution)/shard_map/ppermute | solution.py:131
  4.1 13.4 %collective-permute-start.1 = (bf16[1,256,1024]{2,1,0:T(8,128)(2,1)S(1)}, bf16[1,256,1024]{2,1,0:T(8,128)(2,1)}, u32[]{:S(2)}, u32[]{:S(2)}) collective-permute-start(bf16[1,256,1024]{2,1,0:T(8,128)(2,1)S(1)} %constant_dynamic-update-slice_fusion), channel_id=1, source_target_pairs={{0,1},{1,2},{2,3},{4,5},{5,6},{6,7},{8,9},{9,10},{10,11},{12,13},{... | collective-permute-start | bytes 1572872 | tf_op jit(solution)/shard_map/ppermute | solution.py:131
  18.6 1.6 copy-start.1
  47.5 13.3 %collective-permute-start.4 = (bf16[1,256,512]{2,1,0:T(8,128)(2,1)S(1)}, bf16[1,256,512]{2,1,0:T(8,128)(2,1)S(1)}, u32[]{:S(2)}, u32[]{:S(2)}) collective-permute-start(bf16[1,256,512]{2,1,0:T(8,128)(2,1)S(1)} %get-tuple-element.25), channel_id=1, source_target_pairs={{2,0},{3,1},{6,4},{7,5},{10,8},{11,9},{14,12},{15,13},{18,16},{19,... | collective-permute-start | bytes 786440 | tf_op jit(solution)/shard_map/ppermute | solution.py:183
  55.5 5.3 %collective-permute-start.5 = (bf16[1,256,512]{2,1,0:T(8,128)(2,1)S(1)}, bf16[1,256,512]{2,1,0:T(8,128)(2,1)S(1)}, u32[]{:S(2)}, u32[]{:S(2)}) collective-permute-start(bf16[1,256,512]{2,1,0:T(8,128)(2,1)S(1)} %get-tuple-element.26), channel_id=1, source_target_pairs={{1,0},{2,1},{3,2},{5,4},{6,5},{7,6},{9,8},{10,9},{11,10},{13,12},{... | collective-permute-start | bytes 786440 | tf_op jit(solution)/shard_map/ppermute | solution.py:183
  60.9 72.3 %copy-start.2 = (bf16[1,256,512]{2,1,0:T(8,128)(2,1)}, bf16[1,256,512]{2,1,0:T(8,128)(2,1)S(1)}, u32[]{:S(2)}) copy-start(bf16[1,256,512]{2,1,0:T(8,128)(2,1)S(1)} %fusion.14) | copy-start | bytes 786436
  60.9 6.6 %collective-permute-start.13 = (bf16[256,512]{1,0:T(8,128)(2,1)S(1)}, bf16[256,512]{1,0:T(8,128)(2,1)S(1)}, u32[]{:S(2)}, u32[]{:S(2)}) collective-permute-start(bf16[256,512]{1,0:T(8,128)(2,1)S(1)} %bitcast.54), channel_id=1, source_target_pairs={{0,4},{1,5},{2,6},{3,7},{4,0},{5,1},{6,2},{7,3},{8,12},{9,13},{10,... | collective-permute-start | bytes 786440 | tf_op jit(solution)/shard_map/ppermute | solution.py:194
  67.6 21.3 %copy-start.3 = (bf16[256,512]{1,0:T(8,128)(2,1)}, bf16[256,512]{1,0:T(8,128)(2,1)S(1)}, u32[]{:S(2)}) copy-start(bf16[256,512]{1,0:T(8,128)(2,1)S(1)} %collective-permute-done.13) | copy-start | bytes 786436
  68.5 17.6 %collective-permute-start.14 = (bf16[512,512]{1,0:T(8,128)(2,1)}, bf16[512,512]{1,0:T(8,128)(2,1)}, u32[]{:S(2)}, u32[]{:S(2)}) collective-permute-start(bf16[512,512]{1,0:T(8,128)(2,1)} %pad_maximum_fusion.1), channel_id=1, source_target_pairs={{0,2},{1,3},{2,0},{3,1},{4,6},{5,7},{6,4},{7,5},{8,10},{9,11},{10,... | collective-permute-start | bytes 1572872 | tf_op jit(solution)/shard_map/ppermute | solution.py:194
  78.0 14.1 %collective-permute-start.6 = (bf16[256,1024]{0,1:T(8,128)(2,1)}, bf16[256,1024]{0,1:T(8,128)(2,1)}, u32[]{:S(2)}, u32[]{:S(2)}) collective-permute-start(bf16[256,1024]{0,1:T(8,128)(2,1)} %bitcast.13), channel_id=1, source_target_pairs={{0,4},{1,5},{2,6},{3,7},{4,0},{5,1},{6,2},{7,3},{8,12},{9,13},{10,... | collective-permute-start | bytes 1572872 | tf_op jit(solution)/shard_map/ppermute | solution.py:157
  79.3 18.0 %collective-permute-start.7 = (bf16[256,1024]{0,1:T(8,128)(2,1)}, bf16[256,1024]{0,1:T(8,128)(2,1)S(1)}, u32[]{:S(2)}, u32[]{:S(2)}) collective-permute-start(bf16[256,1024]{0,1:T(8,128)(2,1)} %bitcast.14), channel_id=1, source_target_pairs={{0,2},{1,3},{2,0},{3,1},{4,6},{5,7},{6,4},{7,5},{8,10},{9,11},{10,... | collective-permute-start | bytes 1572872 | tf_op jit(solution)/shard_map/ppermute | solution.py:157
  79.3 30.2 %collective-permute-start.8 = (bf16[256,1024]{0,1:T(8,128)(2,1)}, bf16[256,1024]{0,1:T(8,128)(2,1)S(1)}, u32[]{:S(2)}, u32[]{:S(2)}) collective-permute-start(bf16[256,1024]{0,1:T(8,128)(2,1)} %bitcast.15), channel_id=1, source_target_pairs={{0,6},{1,7},{2,4},{3,5},{4,2},{5,3},{6,0},{7,1},{8,14},{9,15},{10,... | collective-permute-start | bytes 1572872 | tf_op jit(solution)/shard_map/ppermute | solution.py:157
  80.7 31.5 %collective-permute-start.9 = (bf16[256,1024]{0,1:T(8,128)(2,1)}, bf16[256,1024]{0,1:T(8,128)(2,1)S(1)}, u32[]{:S(2)}, u32[]{:S(2)}) collective-permute-start(bf16[256,1024]{0,1:T(8,128)(2,1)} %bitcast.16), channel_id=1, source_target_pairs={{0,1},{1,0},{2,3},{3,2},{4,5},{5,4},{6,7},{7,6},{8,9},{9,8},{10,11... | collective-permute-start | bytes 1572872 | tf_op jit(solution)/shard_map/ppermute | solution.py:157
  81.5 27.9 %copy-start.5 = (bf16[256,4,1,256]{0,3,2,1:T(8,128)(2,1)S(1)}, bf16[256,4,1,256]{0,3,2,1:T(8,128)(2,1)}, u32[]{:S(2)}) copy-start(bf16[256,4,1,256]{0,3,2,1:T(8,128)(2,1)} %get-tuple-element.14) | copy-start | bytes 1572868
  86.1 31.6 %collective-permute-start.10 = (bf16[256,1024]{0,1:T(8,128)(2,1)}, bf16[256,1024]{0,1:T(8,128)(2,1)S(1)}, u32[]{:S(2)}, u32[]{:S(2)}) collective-permute-start(bf16[256,1024]{0,1:T(8,128)(2,1)} %bitcast.61), channel_id=1, source_target_pairs={{0,5},{1,4},{2,7},{3,6},{4,1},{5,0},{6,3},{7,2},{8,13},{9,12},{10,... | collective-permute-start | bytes 1572872 | tf_op jit(solution)/shard_map/ppermute | solution.py:157
  92.1 41.1 %collective-permute-start.15 = (bf16[1024,512]{1,0:T(8,128)(2,1)S(1)}, bf16[1024,512]{1,0:T(8,128)(2,1)S(1)}, u32[]{:S(2)}, u32[]{:S(2)}) collective-permute-start(bf16[1024,512]{1,0:T(8,128)(2,1)S(1)} %pad_maximum_fusion), channel_id=1, source_target_pairs={{0,1},{1,0},{2,3},{3,2},{4,5},{5,4},{6,7},{7,6},{8,9},{9,8},{10,11... | collective-permute-start | bytes 3145736 | tf_op jit(solution)/shard_map/ppermute | solution.py:194
  92.1 41.1 %copy-start.4 = (bf16[256,512]{1,0:T(8,128)(2,1)S(1)}, bf16[256,512]{1,0:T(8,128)(2,1)}, u32[]{:S(2)}) copy-start(bf16[256,512]{1,0:T(8,128)(2,1)} %copy-done.3) | copy-start | bytes 786436
  97.2 23.8 %collective-permute-start.11 = (bf16[256,1024]{0,1:T(8,128)(2,1)}, bf16[256,1024]{0,1:T(8,128)(2,1)S(1)}, u32[]{:S(2)}, u32[]{:S(2)}) collective-permute-start(bf16[256,1024]{0,1:T(8,128)(2,1)} %bitcast.60), channel_id=1, source_target_pairs={{0,3},{1,2},{2,1},{3,0},{4,7},{5,6},{6,5},{7,4},{8,11},{9,10},{10,... | collective-permute-start | bytes 1572872 | tf_op jit(solution)/shard_map/ppermute | solution.py:157
  109.5 22.8 %collective-permute-start.12 = (bf16[256,1024]{0,1:T(8,128)(2,1)S(1)}, bf16[256,1024]{0,1:T(8,128)(2,1)S(1)}, u32[]{:S(2)}, u32[]{:S(2)}) collective-permute-start(bf16[256,1024]{0,1:T(8,128)(2,1)S(1)} %bitcast.59), channel_id=1, source_target_pairs={{0,7},{1,6},{2,5},{3,4},{4,3},{5,2},{6,1},{7,0},{8,15},{9,14},{10,... | collective-permute-start | bytes 1572872 | tf_op jit(solution)/shard_map/ppermute | solution.py:157
  112.2 29.7 %collective-permute-start.2 = (bf16[1,256,512]{2,1,0:T(8,128)(2,1)}, bf16[1,256,512]{2,1,0:T(8,128)(2,1)}, u32[]{:S(2)}, u32[]{:S(2)}) collective-permute-start(bf16[1,256,512]{2,1,0:T(8,128)(2,1)} %get-tuple-element.27), channel_id=1, source_target_pairs={{2,0},{3,1},{6,4},{7,5},{10,8},{11,9},{14,12},{15,13},{18,16},{19,... | collective-permute-start | bytes 786440 | tf_op jit(solution)/shard_map/ppermute | solution.py:183
  117.7 24.2 %collective-permute-start.3 = (bf16[1,256,512]{2,1,0:T(8,128)(2,1)}, bf16[1,256,512]{2,1,0:T(8,128)(2,1)}, u32[]{:S(2)}, u32[]{:S(2)}) collective-permute-start(bf16[1,256,512]{2,1,0:T(8,128)(2,1)} %get-tuple-element.28), channel_id=1, source_target_pairs={{1,0},{2,1},{3,2},{5,4},{6,5},{7,6},{9,8},{10,9},{11,10},{13,12},{... | collective-permute-start | bytes 786440 | tf_op jit(solution)/shard_map/ppermute | solution.py:183
  138.0 8.1 %collective-permute-start.16 = (bf16[256,512]{1,0:T(8,128)(2,1)S(1)}, bf16[256,512]{1,0:T(8,128)(2,1)}, u32[]{:S(2)}, u32[]{:S(2)}) collective-permute-start(bf16[256,512]{1,0:T(8,128)(2,1)S(1)} %get-tuple-element.22), channel_id=1, source_target_pairs={{0,8},{4,12},{8,16},{12,20},{16,24},{20,28},{24,0},{28,4},{1,9},{5... | collective-permute-start | bytes 786440 | tf_op jit(solution)/shard_map/ppermute | solution.py:207
  139.4 22.5 %collective-permute-start.17 = (bf16[256,512]{1,0:T(8,128)(2,1)S(1)}, bf16[256,512]{1,0:T(8,128)(2,1)}, u32[]{:S(2)}, u32[]{:S(2)}) collective-permute-start(bf16[256,512]{1,0:T(8,128)(2,1)S(1)} %get-tuple-element.24), channel_id=1, source_target_pairs={{0,16},{4,20},{8,24},{12,28},{16,0},{20,4},{24,8},{28,12},{1,17},{... | collective-permute-start | bytes 786440 | tf_op jit(solution)/shard_map/ppermute | solution.py:207
  140.5 23.7 %collective-permute-start.18 = (bf16[256,512]{1,0:T(8,128)(2,1)S(1)}, bf16[256,512]{1,0:T(8,128)(2,1)}, u32[]{:S(2)}, u32[]{:S(2)}) collective-permute-start(bf16[256,512]{1,0:T(8,128)(2,1)S(1)} %get-tuple-element.23), channel_id=1, source_target_pairs={{0,24},{4,28},{8,0},{12,4},{16,8},{20,12},{24,16},{28,20},{1,25},{... | collective-permute-start | bytes 786440 | tf_op jit(solution)/shard_map/ppermute | solution.py:207

commit v3 on v2

--- a/solution.py
+++ b/solution.py
@@ -156,8 +156,6 @@
     inputs = [columns_of(member)] + [
         lax.ppermute(columns_of(jnp.bitwise_xor(member, t)), both, flip(t)) for t in order[1:]
     ]
-    all_inputs = jnp.concatenate(inputs, axis=0)
-
     positions = jnp.arange(full_len, dtype=jnp.int32)
     samples = jnp.arange(lengths.shape[1], dtype=jnp.int32)
     ends = jnp.sum(jnp.where(samples[None, :] <= samples[:, None], lengths[:, None, :], 0), axis=2)
@@ -185,6 +183,8 @@
                 ).astype(jnp.float32)
         return total.astype(jnp.bfloat16)
 
+    value_prior, *inputs = lax.optimization_barrier((value_prior, *inputs))
+    all_inputs = jnp.concatenate(inputs, axis=0)
     value_grad = collect(value_own, value_prior)
     key_grad = collect(key_own, key_prior)
 

time: 167 us -> 156 us (0.934)
  the two profiles are of different devices: /device:TPU:15 before, /device:TPU:3 now
where the time goes in v3:
time: 156 us
  waiting for transfers between devices  49.9 us (32%)
  starting transfers between devices  47.7 us (31%)
  Pallas kernels  27.3 us (18%)
  local copies, waits for them, and re-layouts  19.8 us (13%)
  other arithmetic  6.55 us (4%)
  matrix products  3.37 us (2%)
    pallas_call x1, Pallas kernels, attention_grads(): pl.pallas_call(functools.partial(attention_kernel, prior, group), grid=(k...  27.3 us
    ppermute x7, starting transfers between devices, shards(): lax.ppermute(columns_of(jnp.bitwise_xor(member, t)), both, flip(t))  25.5 us
    ppermute x3, waiting for transfers between devices, shards(): lax.ppermute(block, 'dp', turn).astype(jnp.float32)  20.8 us
    ppermute x3, waiting for transfers between devices, shards(): received = lax.ppermute(all_values, both, flip(bit))  18.7 us
    unnamed x35, local copies, waits for them, and re-layouts  12.5 us
    ppermute x4, starting transfers between devices, collect(): lax.ppermute(block, 'seq', [(i + s, i) for i in range(seq_count - s)])  11.8 us
    ppermute x4, waiting for transfers between devices, collect(): lax.ppermute(block, 'seq', [(i + s, i) for i in range(seq_count - s)])  6 us
    dynamic_slice x1, local copies, waits for them, and re-layouts, columns_of(): block = lax.dynamic_slice_in_dim(split_input, owner, 1, axis=2)  4.36 us
  transfers between devices with their start and end apart: 19, of which 7 were waited for; matrix products, arithmetic and copies ran while one was open for 15% of the time, Pallas kernels for 18%

profile of v3, /device:TPU:3, one launch (start us, length us, event | category | flops | bytes accessed | tf_op | source)
XLA Modules:
  0.0 155.7 jit_solution(14209485219228590658)
XLA Ops:
  0.6 1.0 constant_dynamic-update-slice_fusion.1
  1.6 1.0 constant_dynamic-update-slice_fusion
  2.6 1.3 collective-permute-start.1
  3.9 1.3 collective-permute-start
  5.2 6.4 %copy.14 = bf16[1,256,8192]{1,2,0:T(8,128)(2,1)} copy(bf16[1,256,8192]{2,1,0:T(8,128)(2,1)} %param.10) | data formatting | bytes 8388608 | tf_op args[4]
  11.6 4.4 %constant_dynamic-slice_fusion = (bf16[256,4,1,256]{0,3,2,1:T(8,128)(2,1)}, bf16[256,4,1,256]{0,3,2,1:T(8,128)(2,1)}, bf16[256,4,1,256]{0,3,2,1:T(8,128)(2,1)}, ...) fusion(bf16[256,4,8,256]{0,3,2,1:T(8,128)(2,1)} %bitcast.51, ...), kind=kLoop, calls=%fused_computation.40 | loop fusion | bytes 8388640 | tf_op jit(solution)/shard_map/dynamic_slice | solution.py:144
  16.0 1.2 collective-permute-start.4
  17.2 3.4 %collective-permute-start.5 = (bf16[256,1024]{0,1:T(8,128)(2,1)}, bf16[256,1024]{0,1:T(8,128)(2,1)}, u32[]{:S(2)}, u32[]{:S(2)}) collective-permute-start(bf16[256,1024]{0,1:T(8,128)(2,1)} %bitcast.14), channel_id=1, source_target_pairs={{0,2},{1,3},{2,0},{3,1},{4,6},{5,7},{6,4},{7,5},{8,10},{9,11},{10,... | collective-permute-start | bytes 1572872 | tf_op jit(solution)/shard_map/ppermute | solution.py:157
  20.6 0.1 select_reduce_fusion
  20.7 0.1 convert_reduce_fusion
  20.9 0.2 copy.13.sk_ref
  21.1 1.6 %collective-permute-start.7 = (bf16[256,1024]{0,1:T(8,128)(2,1)}, bf16[256,1024]{0,1:T(8,128)(2,1)S(1)}, u32[]{:S(2)}, u32[]{:S(2)}) collective-permute-start(bf16[256,1024]{0,1:T(8,128)(2,1)} %bitcast.62), channel_id=1, source_target_pairs={{0,1},{1,0},{2,3},{3,2},{4,5},{5,4},{6,7},{7,6},{8,9},{9,8},{10,11... | collective-permute-start | bytes 1572872 | tf_op jit(solution)/shard_map/ppermute | solution.py:157
  22.7 3.0 %collective-permute-done = bf16[1,256,1024]{2,1,0:T(8,128)(2,1)} collective-permute-done((bf16[1,256,1024]{2,1,0:T(8,128)(2,1)S(1)}, bf16[1,256,1024]{2,1,0:T(8,128)(2,1)}, u32[]{:S(2)}, u32[]{:S(2)}) %collective-permute-start) | collective-permute-done | bytes 524320 | tf_op jit(solution)/shard_map/ppermute | solution.py:131
  25.7 1.2 maximum_bitcast_fusion.k_ref.v_ref
  26.9 1.5 collective-permute-done.4
  28.4 18.3 %collective-permute-start.9 = (bf16[256,1024]{0,1:T(8,128)(2,1)}, bf16[256,1024]{0,1:T(8,128)(2,1)S(1)}, u32[]{:S(2)}, u32[]{:S(2)}) collective-permute-start(bf16[256,1024]{0,1:T(8,128)(2,1)} %bitcast.60), channel_id=1, source_target_pairs={{0,3},{1,2},{2,1},{3,0},{4,7},{5,6},{6,5},{7,4},{8,11},{9,10},{10,... | collective-permute-start | bytes 1572872 | tf_op jit(solution)/shard_map/ppermute | solution.py:157
  46.7 1.0 collective-permute-start.10
  47.7 1.6 %copy-done.1 = bf16[1,256,4096]{2,1,0:T(8,128)(2,1)S(1)} copy-done((bf16[1,256,4096]{2,1,0:T(8,128)(2,1)S(1)}, bf16[1,256,4096]{2,1,0:T(8,128)(2,1)}, u32[]{:S(2)}) %copy-start.1) | copy-done | bytes 2097176
  49.2 27.3 %shard_map.93 = (bf16[256,4096]{1,0:T(8,128)(2,1)}, bf16[512,512]{1,0:T(8,128)(2,1)S(1)}, bf16[512,512]{1,0:T(8,128)(2,1)S(1)}, f32[256,512]{1,0:T(8,128)S(1)}, f32[256,512]{1,0:T(8,128)S(1)}) custom-call(bf16[256,4096]{1,0:T(8,128)(2,1)S(1)} %bitcast.49, bf16[256,4096]{1,0:T(8,128)(2,1)S(1)} %bitcast.50, ...), custom_call_target="tpu_custom_call" | custom-call | flops 8053063680 | bytes 10485760 | tf_op jit(solution)/shard_map/pallas_call | solution.py:80
  76.7 1.4 collective-permute-start.12
  78.1 4.4 %collective-permute-start.11 = (bf16[1,256,512]{2,1,0:T(8,128)(2,1)S(1)}, bf16[1,256,512]{2,1,0:T(8,128)(2,1)S(1)}, u32[]{:S(2)}, u32[]{:S(2)}) collective-permute-start(bf16[1,256,512]{2,1,0:T(8,128)(2,1)S(1)} %get-tuple-element.43), channel_id=1, source_target_pairs={{2,0},{3,1},{6,4},{7,5},{10,8},{11,9},{14,12},{15,13},{18,16},{19,... | collective-permute-start | bytes 786440 | tf_op jit(solution)/shard_map/ppermute | solution.py:181
  82.5 6.0 %collective-permute-done.11 = bf16[1,256,512]{2,1,0:T(8,128)(2,1)S(1)} collective-permute-done((bf16[1,256,512]{2,1,0:T(8,128)(2,1)S(1)}, bf16[1,256,512]{2,1,0:T(8,128)(2,1)S(1)}, u32[]{:S(2)}, u32[]{:S(2)}) %collective-permute-start.11) | collective-permute-done | bytes 262176 | tf_op jit(solution)/shard_map/ppermute | solution.py:181
  88.5 0.1 fusion.14
  88.6 0.3 collective-permute-start.13
  88.9 7.5 %collective-permute-done.13 = bf16[256,512]{1,0:T(8,128)(2,1)S(1)} collective-permute-done((bf16[256,512]{1,0:T(8,128)(2,1)S(1)}, bf16[256,512]{1,0:T(8,128)(2,1)S(1)}, u32[]{:S(2)}, u32[]{:S(2)}) %collective-permute-start.13) | collective-permute-done | bytes 262176 | tf_op jit(solution)/shard_map/ppermute | solution.py:194
  96.5 1.8 %collective-permute-start.14 = (bf16[512,512]{1,0:T(8,128)(2,1)S(1)}, bf16[512,512]{1,0:T(8,128)(2,1)}, u32[]{:S(2)}, u32[]{:S(2)}) collective-permute-start(bf16[512,512]{1,0:T(8,128)(2,1)S(1)} %pad_maximum_fusion.1), channel_id=1, source_target_pairs={{0,2},{1,3},{2,0},{3,1},{4,6},{5,7},{6,4},{7,5},{8,10},{9,11},{10,... | collective-permute-start | bytes 1572872 | tf_op jit(solution)/shard_map/ppermute | solution.py:194
  98.3 11.1 %collective-permute-done.14 = bf16[512,512]{1,0:T(8,128)(2,1)} collective-permute-done((bf16[512,512]{1,0:T(8,128)(2,1)S(1)}, bf16[512,512]{1,0:T(8,128)(2,1)}, u32[]{:S(2)}, u32[]{:S(2)}) %collective-permute-start.14) | collective-permute-done | bytes 524320 | tf_op jit(solution)/shard_map/ppermute | solution.py:194
  109.4 1.1 pad_maximum_fusion
  110.5 1.9 %collective-permute-start.15 = (bf16[1024,512]{1,0:T(8,128)(2,1)S(1)}, bf16[1024,512]{1,0:T(8,128)(2,1)S(1)}, u32[]{:S(2)}, u32[]{:S(2)}) collective-permute-start(bf16[1024,512]{1,0:T(8,128)(2,1)S(1)} %pad_maximum_fusion), channel_id=1, source_target_pairs={{0,1},{1,0},{2,3},{3,2},{4,5},{5,4},{6,7},{7,6},{8,9},{9,8},{10,11... | collective-permute-start | bytes 3145736 | tf_op jit(solution)/shard_map/ppermute | solution.py:194
  112.5 0.8 fusion.20
  113.3 1.9 %collective-permute-start.3 = (bf16[1,256,512]{2,1,0:T(8,128)(2,1)}, bf16[1,256,512]{2,1,0:T(8,128)(2,1)S(1)}, u32[]{:S(2)}, u32[]{:S(2)}) collective-permute-start(bf16[1,256,512]{2,1,0:T(8,128)(2,1)} %get-tuple-element.46), channel_id=1, source_target_pairs={{1,0},{2,1},{3,2},{5,4},{6,5},{7,6},{9,8},{10,9},{11,10},{13,12},{... | collective-permute-start | bytes 786440 | tf_op jit(solution)/shard_map/ppermute | solution.py:181
  115.3 4.1 %collective-permute-start.2 = (bf16[1,256,512]{2,1,0:T(8,128)(2,1)}, bf16[1,256,512]{2,1,0:T(8,128)(2,1)}, u32[]{:S(2)}, u32[]{:S(2)}) collective-permute-start(bf16[1,256,512]{2,1,0:T(8,128)(2,1)} %get-tuple-element.45), channel_id=1, source_target_pairs={{2,0},{3,1},{6,4},{7,5},{10,8},{11,9},{14,12},{15,13},{18,16},{19,... | collective-permute-start | bytes 786440 | tf_op jit(solution)/shard_map/ppermute | solution.py:181
  119.4 1.1 constant_dynamic-update-slice_fusion.8
  120.5 1.1 constant_dynamic-update-slice_fusion.7
  121.6 1.1 constant_dynamic-update-slice_fusion.6
  122.7 0.1 constant_dynamic-update-slice_fusion.5
  122.8 0.1 constant_dynamic-update-slice_fusion.4
  122.9 0.1 constant_dynamic-update-slice_fusion.3
  123.0 0.1 constant_dynamic-update-slice_fusion.2
  123.1 3.4 %fusion.8 = f32[1024,512]{1,0:T(8,128)S(1)} fusion(bf16[2048,1024]{0,1:T(8,128)(2,1)S(1)} %constant_dynamic-update-slice_fusion.2, bf16[1024,512]{1,0:T(8,128)(2,1)S(1)} %collective-permute-done.15, bf16[512,512]{1,0:T(8,128)(2,1)} %collective-permute-done.14, bf16[256,512]{1,0:T(8,128)(2,1)S(1)} %collective-permute-done.13, bf16[256,512]{1,0:T(8,128)(2,1)S(1)} %bitcast.57), kind=kOutput, calls=%fused_computation.8 | convolution fusion | flops 2156396544 | bytes 8388608 | tf_op jit(solution)/shard_map/dot_general | solution.py:197
  126.5 0.1 convert_element_type.48
  126.6 0.8 dynamic-slice_bitcast_fusion.2
  127.4 3.3 %collective-permute-start.18 = (bf16[256,512]{1,0:T(8,128)(2,1)}, bf16[256,512]{1,0:T(8,128)(2,1)}, u32[]{:S(2)}, u32[]{:S(2)}) collective-permute-start(bf16[256,512]{1,0:T(8,128)(2,1)} %get-tuple-element.41), channel_id=1, source_target_pairs={{0,24},{4,28},{8,0},{12,4},{16,8},{20,12},{24,16},{28,20},{1,25},{... | collective-permute-start | bytes 786440 | tf_op jit(solution)/shard_map/ppermute | solution.py:207
  130.7 0.4 collective-permute-start.16
  131.1 1.8 %fusion.16 = bf16[1,256,512]{2,1,0:T(8,128)(2,1)} fusion(f32[256,512]{1,0:T(8,128)S(1)} %get-tuple-element.19, bf16[1,256,512]{2,1,0:T(8,128)(2,1)S(1)} %collective-permute-done.3, bf16[1,256,512]{2,1,0:T(8,128)(2,1)} %collective-permute-done.2), kind=kLoop, calls=%fused_computation.20 | loop fusion | flops 655360 | bytes 1310720 | tf_op jit(solution)/shard_map/convert_element_type | solution.py:184
  132.9 4.1 %collective-permute-done.18 = bf16[256,512]{1,0:T(8,128)(2,1)} collective-permute-done((bf16[256,512]{1,0:T(8,128)(2,1)}, bf16[256,512]{1,0:T(8,128)(2,1)}, u32[]{:S(2)}, u32[]{:S(2)}) %collective-permute-start.18) | collective-permute-done | bytes 262176 | tf_op jit(solution)/shard_map/ppermute | solution.py:207
  137.0 16.7 %collective-permute-done.17 = bf16[256,512]{1,0:T(8,128)(2,1)} collective-permute-done((bf16[256,512]{1,0:T(8,128)(2,1)S(1)}, bf16[256,512]{1,0:T(8,128)(2,1)}, u32[]{:S(2)}, u32[]{:S(2)}) %collective-permute-start.17) | collective-permute-done | bytes 262176 | tf_op jit(solution)/shard_map/ppermute | solution.py:207
  153.7 2.0 %fusion.12 = f32[256,512]{1,0:T(8,128)} fusion(bf16[256,512]{1,0:T(8,128)(2,1)} %collective-permute-done.18, bf16[256,512]{1,0:T(8,128)(2,1)} %collective-permute-done.17, bf16[256,512]{1,0:T(8,128)(2,1)} %collective-permute-done.16, f32[4,256,512]{2,1,0:T(8,128)S(1)} %bitcast.53, s32[]{:T(128)S(6)} %select_n.69), kind=kLoop, calls=%fused_computation.14 | loop fusion | flops 786432 | bytes 1835012 | tf_op jit(solution)/shard_map/add | solution.py:207
  (45 shorter events, 0.3 us)
Async XLA Ops:
  2.6 18.5 %collective-permute-start.1 = (bf16[1,256,1024]{2,1,0:T(8,128)(2,1)S(1)}, bf16[1,256,1024]{2,1,0:T(8,128)(2,1)S(1)}, u32[]{:S(2)}, u32[]{:S(2)}) collective-permute-start(bf16[1,256,1024]{2,1,0:T(8,128)(2,1)S(1)} %constant_dynamic-update-slice_fusion), channel_id=1, source_target_pairs={{0,1},{1,2},{2,3},{4,5},{5,6},{6,7},{8,9},{9,10},{10,11},{12,13},{... | collective-permute-start | bytes 1572872 | tf_op jit(solution)/shard_map/ppermute | solution.py:131
  3.9 21.8 %collective-permute-start = (bf16[1,256,1024]{2,1,0:T(8,128)(2,1)S(1)}, bf16[1,256,1024]{2,1,0:T(8,128)(2,1)}, u32[]{:S(2)}, u32[]{:S(2)}) collective-permute-start(bf16[1,256,1024]{2,1,0:T(8,128)(2,1)S(1)} %constant_dynamic-update-slice_fusion), channel_id=1, source_target_pairs={{0,2},{1,3},{4,6},{5,7},{8,10},{9,11},{12,14},{13,15},{16,18},{17,... | collective-permute-start | bytes 1572872 | tf_op jit(solution)/shard_map/ppermute | solution.py:131
  11.6 9.0 %copy-start.12 = (s32[1,8]{1,0:T(1,128)S(1)}, s32[1,8]{1,0:T(1,128)}, u32[]{:S(2)}) copy-start(s32[1,8]{1,0:T(1,128)} %param.11) | copy-start | bytes 100
  11.6 36.1 %copy-start = (bf16[1,256,4096]{2,1,0:T(8,128)(2,1)S(1)}, bf16[1,256,4096]{2,1,0:T(8,128)(2,1)}, u32[]{:S(2)}) copy-start(bf16[1,256,4096]{2,1,0:T(8,128)(2,1)} %param.6) | copy-start | bytes 6291460
  16.0 12.4 %collective-permute-start.4 = (bf16[256,1024]{0,1:T(8,128)(2,1)}, bf16[256,1024]{0,1:T(8,128)(2,1)}, u32[]{:S(2)}, u32[]{:S(2)}) collective-permute-start(bf16[256,1024]{0,1:T(8,128)(2,1)} %bitcast.13), channel_id=1, source_target_pairs={{0,4},{1,5},{2,6},{3,7},{4,0},{5,1},{6,2},{7,3},{8,12},{9,13},{10,... | collective-permute-start | bytes 1572872 | tf_op jit(solution)/shard_map/ppermute | solution.py:157
  17.2 29.5 %collective-permute-start.5 = (bf16[256,1024]{0,1:T(8,128)(2,1)}, bf16[256,1024]{0,1:T(8,128)(2,1)}, u32[]{:S(2)}, u32[]{:S(2)}) collective-permute-start(bf16[256,1024]{0,1:T(8,128)(2,1)} %bitcast.14), channel_id=1, source_target_pairs={{0,2},{1,3},{2,0},{3,1},{4,6},{5,7},{6,4},{7,5},{8,10},{9,11},{10,... | collective-permute-start | bytes 1572872 | tf_op jit(solution)/shard_map/ppermute | solution.py:157
  20.6 55.9 %collective-permute-start.6 = (bf16[256,1024]{0,1:T(8,128)(2,1)}, bf16[256,1024]{0,1:T(8,128)(2,1)}, u32[]{:S(2)}, u32[]{:S(2)}) collective-permute-start(bf16[256,1024]{0,1:T(8,128)(2,1)} %bitcast.15), channel_id=1, source_target_pairs={{0,6},{1,7},{2,4},{3,5},{4,2},{5,3},{6,0},{7,1},{8,14},{9,15},{10,... | collective-permute-start | bytes 1572872 | tf_op jit(solution)/shard_map/ppermute | solution.py:157
  21.1 55.5 %collective-permute-start.7 = (bf16[256,1024]{0,1:T(8,128)(2,1)}, bf16[256,1024]{0,1:T(8,128)(2,1)S(1)}, u32[]{:S(2)}, u32[]{:S(2)}) collective-permute-start(bf16[256,1024]{0,1:T(8,128)(2,1)} %bitcast.62), channel_id=1, source_target_pairs={{0,1},{1,0},{2,3},{3,2},{4,5},{5,4},{6,7},{7,6},{8,9},{9,8},{10,11... | collective-permute-start | bytes 1572872 | tf_op jit(solution)/shard_map/ppermute | solution.py:157
  25.7 50.8 %collective-permute-start.8 = (bf16[256,1024]{0,1:T(8,128)(2,1)}, bf16[256,1024]{0,1:T(8,128)(2,1)S(1)}, u32[]{:S(2)}, u32[]{:S(2)}) collective-permute-start(bf16[256,1024]{0,1:T(8,128)(2,1)} %bitcast.61), channel_id=1, source_target_pairs={{0,5},{1,4},{2,7},{3,6},{4,1},{5,0},{6,3},{7,2},{8,13},{9,12},{10,... | collective-permute-start | bytes 1572872 | tf_op jit(solution)/shard_map/ppermute | solution.py:157
  28.4 48.2 %collective-permute-start.9 = (bf16[256,1024]{0,1:T(8,128)(2,1)}, bf16[256,1024]{0,1:T(8,128)(2,1)S(1)}, u32[]{:S(2)}, u32[]{:S(2)}) collective-permute-start(bf16[256,1024]{0,1:T(8,128)(2,1)} %bitcast.60), channel_id=1, source_target_pairs={{0,3},{1,2},{2,1},{3,0},{4,7},{5,6},{6,5},{7,4},{8,11},{9,10},{10,... | collective-permute-start | bytes 1572872 | tf_op jit(solution)/shard_map/ppermute | solution.py:157
  46.7 29.9 %collective-permute-start.10 = (bf16[256,1024]{0,1:T(8,128)(2,1)}, bf16[256,1024]{0,1:T(8,128)(2,1)S(1)}, u32[]{:S(2)}, u32[]{:S(2)}) collective-permute-start(bf16[256,1024]{0,1:T(8,128)(2,1)} %bitcast.59), channel_id=1, source_target_pairs={{0,7},{1,6},{2,5},{3,4},{4,3},{5,2},{6,1},{7,0},{8,15},{9,14},{10,... | collective-permute-start | bytes 1572872 | tf_op jit(solution)/shard_map/ppermute | solution.py:157
  47.7 1.6 %copy-start.1 = (bf16[1,256,4096]{2,1,0:T(8,128)(2,1)S(1)}, bf16[1,256,4096]{2,1,0:T(8,128)(2,1)}, u32[]{:S(2)}) copy-start(bf16[1,256,4096]{2,1,0:T(8,128)(2,1)} %param.9) | copy-start | bytes 6291460
  76.5 42.8 %copy-start.3 = (bf16[256,4,1,256]{0,3,2,1:T(8,128)(2,1)S(1)}, bf16[256,4,1,256]{0,3,2,1:T(8,128)(2,1)}, u32[]{:S(2)}) copy-start(bf16[256,4,1,256]{0,3,2,1:T(8,128)(2,1)} %get-tuple-element.39) | copy-start | bytes 1572868
  76.5 19.9 %copy-start.4 = (bf16[256,1024]{0,1:T(8,128)(2,1)}, bf16[256,1024]{0,1:T(8,128)(2,1)S(1)}, u32[]{:S(2)}) copy-start(bf16[256,1024]{0,1:T(8,128)(2,1)S(1)} %collective-permute-done.7) | copy-start | bytes 1572868
  76.6 19.9 %copy-start.6 = (bf16[256,1024]{0,1:T(8,128)(2,1)}, bf16[256,1024]{0,1:T(8,128)(2,1)S(1)}, u32[]{:S(2)}) copy-start(bf16[256,1024]{0,1:T(8,128)(2,1)S(1)} %collective-permute-done.8) | copy-start | bytes 1572868
  76.6 19.9 %copy-start.8 = (bf16[256,1024]{0,1:T(8,128)(2,1)}, bf16[256,1024]{0,1:T(8,128)(2,1)S(1)}, u32[]{:S(2)}) copy-start(bf16[256,1024]{0,1:T(8,128)(2,1)S(1)} %collective-permute-done.9) | copy-start | bytes 1572868
  76.6 19.9 %copy-start.10 = (bf16[256,1024]{0,1:T(8,128)(2,1)}, bf16[256,1024]{0,1:T(8,128)(2,1)S(1)}, u32[]{:S(2)}) copy-start(bf16[256,1024]{0,1:T(8,128)(2,1)S(1)} %collective-permute-done.10) | copy-start | bytes 1572868
  76.7 5.8 %collective-permute-start.12 = (bf16[1,256,512]{2,1,0:T(8,128)(2,1)S(1)}, bf16[1,256,512]{2,1,0:T(8,128)(2,1)S(1)}, u32[]{:S(2)}, u32[]{:S(2)}) collective-permute-start(bf16[1,256,512]{2,1,0:T(8,128)(2,1)S(1)} %get-tuple-element.44), channel_id=1, source_target_pairs={{1,0},{2,1},{3,2},{5,4},{6,5},{7,6},{9,8},{10,9},{11,10},{13,12},{... | collective-permute-start | bytes 786440 | tf_op jit(solution)/shard_map/ppermute | solution.py:181
  78.1 10.4 %collective-permute-start.11 = (bf16[1,256,512]{2,1,0:T(8,128)(2,1)S(1)}, bf16[1,256,512]{2,1,0:T(8,128)(2,1)S(1)}, u32[]{:S(2)}, u32[]{:S(2)}) collective-permute-start(bf16[1,256,512]{2,1,0:T(8,128)(2,1)S(1)} %get-tuple-element.43), channel_id=1, source_target_pairs={{2,0},{3,1},{6,4},{7,5},{10,8},{11,9},{14,12},{15,13},{18,16},{19,... | collective-permute-start | bytes 786440 | tf_op jit(solution)/shard_map/ppermute | solution.py:181
  88.6 34.4 %copy-start.2 = (bf16[1,256,512]{2,1,0:T(8,128)(2,1)}, bf16[1,256,512]{2,1,0:T(8,128)(2,1)S(1)}, u32[]{:S(2)}) copy-start(bf16[1,256,512]{2,1,0:T(8,128)(2,1)S(1)} %fusion.14) | copy-start | bytes 786436
  88.6 7.8 %collective-permute-start.13 = (bf16[256,512]{1,0:T(8,128)(2,1)S(1)}, bf16[256,512]{1,0:T(8,128)(2,1)S(1)}, u32[]{:S(2)}, u32[]{:S(2)}) collective-permute-start(bf16[256,512]{1,0:T(8,128)(2,1)S(1)} %bitcast.54), channel_id=1, source_target_pairs={{0,4},{1,5},{2,6},{3,7},{4,0},{5,1},{6,2},{7,3},{8,12},{9,13},{10,... | collective-permute-start | bytes 786440 | tf_op jit(solution)/shard_map/ppermute | solution.py:194
  96.5 12.9 %collective-permute-start.14 = (bf16[512,512]{1,0:T(8,128)(2,1)S(1)}, bf16[512,512]{1,0:T(8,128)(2,1)}, u32[]{:S(2)}, u32[]{:S(2)}) collective-permute-start(bf16[512,512]{1,0:T(8,128)(2,1)S(1)} %pad_maximum_fusion.1), channel_id=1, source_target_pairs={{0,2},{1,3},{2,0},{3,1},{4,6},{5,7},{6,4},{7,5},{8,10},{9,11},{10,... | collective-permute-start | bytes 1572872 | tf_op jit(solution)/shard_map/ppermute | solution.py:194
  98.3 24.4 %copy-start.5 = (bf16[256,1024]{0,1:T(8,128)(2,1)S(1)}, bf16[256,1024]{0,1:T(8,128)(2,1)}, u32[]{:S(2)}) copy-start(bf16[256,1024]{0,1:T(8,128)(2,1)} %copy-done.4) | copy-start | bytes 1572868
  98.3 24.5 %copy-start.7 = (bf16[256,1024]{0,1:T(8,128)(2,1)S(1)}, bf16[256,1024]{0,1:T(8,128)(2,1)}, u32[]{:S(2)}) copy-start(bf16[256,1024]{0,1:T(8,128)(2,1)} %copy-done.6) | copy-start | bytes 1572868
  110.5 12.4 %copy-start.9 = (bf16[256,1024]{0,1:T(8,128)(2,1)S(1)}, bf16[256,1024]{0,1:T(8,128)(2,1)}, u32[]{:S(2)}) copy-start(bf16[256,1024]{0,1:T(8,128)(2,1)} %copy-done.8) | copy-start | bytes 1572868
  110.5 12.5 %collective-permute-start.15 = (bf16[1024,512]{1,0:T(8,128)(2,1)S(1)}, bf16[1024,512]{1,0:T(8,128)(2,1)S(1)}, u32[]{:S(2)}, u32[]{:S(2)}) collective-permute-start(bf16[1024,512]{1,0:T(8,128)(2,1)S(1)} %pad_maximum_fusion), channel_id=1, source_target_pairs={{0,1},{1,0},{2,3},{3,2},{4,5},{5,4},{6,7},{7,6},{8,9},{9,8},{10,11... | collective-permute-start | bytes 3145736 | tf_op jit(solution)/shard_map/ppermute | solution.py:194
  112.5 10.5 %copy-start.11 = (bf16[256,1024]{0,1:T(8,128)(2,1)S(1)}, bf16[256,1024]{0,1:T(8,128)(2,1)}, u32[]{:S(2)}) copy-start(bf16[256,1024]{0,1:T(8,128)(2,1)} %copy-done.10) | copy-start | bytes 1572868
  113.3 17.8 %collective-permute-start.3 = (bf16[1,256,512]{2,1,0:T(8,128)(2,1)}, bf16[1,256,512]{2,1,0:T(8,128)(2,1)S(1)}, u32[]{:S(2)}, u32[]{:S(2)}) collective-permute-start(bf16[1,256,512]{2,1,0:T(8,128)(2,1)} %get-tuple-element.46), channel_id=1, source_target_pairs={{1,0},{2,1},{3,2},{5,4},{6,5},{7,6},{9,8},{10,9},{11,10},{13,12},{... | collective-permute-start | bytes 786440 | tf_op jit(solution)/shard_map/ppermute | solution.py:181
  115.3 15.9 %collective-permute-start.2 = (bf16[1,256,512]{2,1,0:T(8,128)(2,1)}, bf16[1,256,512]{2,1,0:T(8,128)(2,1)}, u32[]{:S(2)}, u32[]{:S(2)}) collective-permute-start(bf16[1,256,512]{2,1,0:T(8,128)(2,1)} %get-tuple-element.45), channel_id=1, source_target_pairs={{2,0},{3,1},{6,4},{7,5},{10,8},{11,9},{14,12},{15,13},{18,16},{19,... | collective-permute-start | bytes 786440 | tf_op jit(solution)/shard_map/ppermute | solution.py:181
  127.4 9.6 %collective-permute-start.18 = (bf16[256,512]{1,0:T(8,128)(2,1)}, bf16[256,512]{1,0:T(8,128)(2,1)}, u32[]{:S(2)}, u32[]{:S(2)}) collective-permute-start(bf16[256,512]{1,0:T(8,128)(2,1)} %get-tuple-element.41), channel_id=1, source_target_pairs={{0,24},{4,28},{8,0},{12,4},{16,8},{20,12},{24,16},{28,20},{1,25},{... | collective-permute-start | bytes 786440 | tf_op jit(solution)/shard_map/ppermute | solution.py:207
  130.7 23.0 %collective-permute-start.17 = (bf16[256,512]{1,0:T(8,128)(2,1)S(1)}, bf16[256,512]{1,0:T(8,128)(2,1)}, u32[]{:S(2)}, u32[]{:S(2)}) collective-permute-start(bf16[256,512]{1,0:T(8,128)(2,1)S(1)} %get-tuple-element.42), channel_id=1, source_target_pairs={{0,16},{4,20},{8,24},{12,28},{16,0},{20,4},{24,8},{28,12},{1,17},{... | collective-permute-start | bytes 786440 | tf_op jit(solution)/shard_map/ppermute | solution.py:207
  130.7 23.0 %collective-permute-start.16 = (bf16[256,512]{1,0:T(8,128)(2,1)S(1)}, bf16[256,512]{1,0:T(8,128)(2,1)}, u32[]{:S(2)}, u32[]{:S(2)}) collective-permute-start(bf16[256,512]{1,0:T(8,128)(2,1)S(1)} %get-tuple-element.40), channel_id=1, source_target_pairs={{0,8},{4,12},{8,16},{12,20},{16,24},{20,28},{24,0},{28,4},{1,9},{5... | collective-permute-start | bytes 786440 | tf_op jit(solution)/shard_map/ppermute | solution.py:207
